TPU v7x, 32 devices: a whole 2x2x4 slice. The times are simulated.
32 devices in a mesh: batch: 2 (over x), pos: 8 (over z, core), ch: 2 (over y).
Axes of the slice: x: 2, y: 2, z: 4, core: 2. Of those that a mesh axis runs over, the one named last changes fastest.
Arguments:
- section_input: bfloat16 [2, 2, 8192, 1280], P(None, 'batch', 'pos', 'ch')
- norm1_gain: float32 [1280], P('ch'), may hold values from 0.1 to 1.9
- norm1_bias: float32 [1280], P('ch'), may hold values from -3 to 3
- conv1_weight: bfloat16 [6400, 1536], P(None, 'ch'), may hold values from -0.078125 to 0.078125
- conv1_bias: float32 [1536], P('ch'), may hold values from -3 to 3
- norm2_gain: float32 [1536], P('ch'), may hold values from 0.1 to 1.9
- norm2_bias: float32 [1536], P('ch'), may hold values from -3 to 3
- conv2_weight: bfloat16 [1536, 1536], P(None, 'ch'), may hold values from -0.15625 to 0.15625
- conv2_bias: float32 [1536], P('ch'), may hold values from -3 to 3
- pool_weight: bfloat16 [1536, 1536], P(None, 'ch'), may hold values from -0.3125 to 0.3125
- out_grad: bfloat16 [2, 2, 4096, 1536], P(None, 'batch', 'pos', 'ch'), may hold values from -8 to 8
- clip_table: float32 [8], replicated, may hold values from 0.5 to 3
- clip_index: int32 [2], replicated, may hold values from 0 to 7
Outputs:
- section_output: bfloat16 [2, 2, 4096, 1536], P(None, 'batch', 'pos', 'ch')
- input_grad: bfloat16 [2, 2, 8192, 1280], P(None, 'batch', 'pos', 'ch')
- grad_norm1_gain: float32 [1280], P('ch')
- grad_norm1_bias: float32 [1280], P('ch')
- grad_conv1_weight: float32 [6400, 1536], P(('batch', 'pos'), 'ch')
- grad_conv1_bias: float32 [1536], P('ch')
- grad_norm2_gain: float32 [1536], P('ch')
- grad_norm2_bias: float32 [1536], P('ch')
- grad_conv2_weight: float32 [1536, 1536], P(('batch', 'pos'), 'ch')
- grad_conv2_bias: float32 [1536], P('ch')
- grad_pool_weight: float32 [1536, 1536], P(('batch', 'pos'), 'ch')
All inputs are finite; a program needn't handle non-finite values.
Results may differ from a plain program's by a relative error of at most 0.017.
Values may be sent and summed in bfloat16 or wider, within the bound.
A program may use at most 384 MiB of HBM per device.

v0:
```python
import jax
import jax.numpy as jnp
from jax import lax
from jax.sharding import PartitionSpec as P

KW = 5


EPS = 1e-05


def extended(array, sides, width):
    for axis, dim in sides:
        size, length = (lax.axis_size(axis), array.shape[dim])
        up = [(i, (i + 1) % size) for i in range(size - 1)]
        down = [(j, i) for i, j in up]
        last = lax.slice_in_dim(array, length - width, length, axis=dim)
        first = lax.slice_in_dim(array, 0, width, axis=dim)
        before = lax.ppermute(last, axis, up)
        after = lax.ppermute(first, axis, down)
        array = jnp.concatenate([before, array, after], axis=dim)
    return array


def moments(values):
    return (jnp.sum(values, axis=(0, 1)), jnp.sum(values * values, axis=(0, 1)))


def standardize(values, sums, total_rows):
    center = sums[0] / total_rows
    inverse = lax.rsqrt(sums[1] / total_rows - center * center + EPS)
    return ((values - center) * inverse, inverse)


def norm_back(act_grad, normed, inverse, gain_vec, grad_sum, cross_sum, total_rows):
    return (
        inverse * gain_vec * (act_grad - grad_sum / total_rows - normed * (cross_sum / total_rows))
    )


def channel_product(left, right):
    return jnp.einsum("slc,co->slo", left, right, preferred_element_type=jnp.float32)


def back_product(left, right):
    return jnp.einsum("slo,co->slc", left, right, preferred_element_type=jnp.float32)


def weight_product(left, right):
    return jnp.einsum("slc,slo->co", left, right, preferred_element_type=jnp.float32)


def pool_pairs(logits, values):
    pair_shape = (values.shape[0], values.shape[1] // 2, 2, values.shape[2])
    weights = jax.nn.softmax(logits.reshape(pair_shape), axis=2)
    return jnp.sum(weights * values.reshape(pair_shape), axis=2)


def stack_windows(whole_one, local_rows):
    return jnp.concatenate(
        [whole_one[:, offset : offset + local_rows] for offset in range(KW)], axis=2
    )


def local(
    section_input,
    norm1_gain,
    norm1_bias,
    conv1_weight,
    conv1_bias,
    norm2_gain,
    norm2_bias,
    conv2_weight,
    conv2_bias,
    pool_weight,
    out_grad,
    clip_table,
    clip_index,
):
    micro_count, seq_count, local_rows, local_in = section_input.shape
    rim_width = KW // 2
    pair_count = lax.axis_size("batch")
    total_rows = seq_count * local_rows * pair_count * lax.axis_size("pos")
    wide_in = conv1_weight.shape[0] // KW
    local_out = conv1_weight.shape[1]
    wide_out = conv2_weight.shape[0]
    kernel = conv1_weight.reshape(KW, wide_in, local_out)
    table_pos = jnp.arange(clip_table.shape[0], dtype=jnp.int32)
    accum_one = jnp.zeros((KW * wide_in // pair_count, local_out), jnp.float32)
    accum_two = jnp.zeros((wide_out // pair_count, local_out), jnp.float32)
    accum_pool = jnp.zeros((wide_out // pair_count, local_out), jnp.float32)
    gain_one_grad = jnp.zeros((local_in,), jnp.float32)
    bias_one_grad = jnp.zeros((local_in,), jnp.float32)
    conv_one_bias_grad = jnp.zeros((local_out,), jnp.float32)
    gain_two_grad = jnp.zeros((local_out,), jnp.float32)
    bias_two_grad = jnp.zeros((local_out,), jnp.float32)
    conv_two_bias_grad = jnp.zeros((local_out,), jnp.float32)
    outputs = []
    input_grads = []
    for micro_step in range(micro_count):
        inputs = section_input[micro_step].astype(jnp.float32)
        sums_one = lax.psum(moments(inputs), ("batch", "pos"))
        normed_one, inverse_one = standardize(inputs, sums_one, total_rows)
        act_one = normed_one * norm1_gain + norm1_bias
        gelu_one, pull_one = jax.vjp(jax.nn.gelu, act_one)
        hidden_one = gelu_one.astype(jnp.bfloat16)
        rim_one = extended(hidden_one, (("pos", 1),), rim_width)
        whole_one = lax.all_gather(rim_one, "ch", axis=2, tiled=True)
        first_out = conv1_bias
        for offset in range(KW):
            first_out = first_out + channel_product(
                whole_one[:, offset : offset + local_rows], kernel[offset]
            )
        sums_two = lax.psum(moments(first_out), ("batch", "pos"))
        normed_two, inverse_two = standardize(first_out, sums_two, total_rows)
        act_two = normed_two * norm2_gain + norm2_bias
        gelu_two, pull_two = jax.vjp(jax.nn.gelu, act_two)
        whole_two = lax.all_gather(gelu_two.astype(jnp.bfloat16), "ch", axis=2, tiled=True)
        second_out = first_out + conv2_bias + channel_product(whole_two, conv2_weight)
        whole_pool = lax.all_gather(second_out.astype(jnp.bfloat16), "ch", axis=2, tiled=True)
        logits = channel_product(whole_pool, pool_weight)
        pooled, pull_pool = jax.vjp(pool_pairs, logits, second_out)
        outputs.append(pooled.astype(jnp.bfloat16))
        limit = jnp.sum(jnp.where(table_pos == clip_index[micro_step], clip_table, 0.0))
        clipped = limit * jnp.tanh(out_grad[micro_step].astype(jnp.float32) / limit)
        logit_grad, value_grad = pull_pool(clipped)
        logit_low = logit_grad.astype(jnp.bfloat16)
        second_grad = value_grad + lax.psum_scatter(
            back_product(logit_low, pool_weight).astype(jnp.bfloat16),
            "ch",
            scatter_dimension=2,
            tiled=True,
        ).astype(jnp.float32)
        branch_grad = second_grad.astype(jnp.bfloat16)
        hidden_two_grad = lax.psum_scatter(
            back_product(branch_grad, conv2_weight).astype(jnp.bfloat16),
            "ch",
            scatter_dimension=2,
            tiled=True,
        ).astype(jnp.float32)
        act_two_grad = pull_two(hidden_two_grad)[0]
        two_sum, two_cross, two_bias = lax.psum(
            (
                jnp.sum(act_two_grad, axis=(0, 1)),
                jnp.sum(act_two_grad * normed_two, axis=(0, 1)),
                jnp.sum(branch_grad.astype(jnp.float32), axis=(0, 1)),
            ),
            ("batch", "pos"),
        )
        gain_two_grad = gain_two_grad + two_cross
        bias_two_grad = bias_two_grad + two_sum
        conv_two_bias_grad = conv_two_bias_grad + two_bias
        first_grad = second_grad + norm_back(
            act_two_grad, normed_two, inverse_two, norm2_gain, two_sum, two_cross, total_rows
        )
        first_low = first_grad.astype(jnp.bfloat16)
        grad_rim = extended(first_low, (("pos", 1),), rim_width)
        partial_one = back_product(
            grad_rim[:, 2 * rim_width : 2 * rim_width + local_rows], kernel[0]
        )
        for offset in range(1, KW):
            begin = 2 * rim_width - offset
            partial_one = partial_one + back_product(
                grad_rim[:, begin : begin + local_rows], kernel[offset]
            )
        hidden_one_grad = lax.psum_scatter(
            partial_one.astype(jnp.bfloat16), "ch", scatter_dimension=2, tiled=True
        ).astype(jnp.float32)
        act_one_grad = pull_one(hidden_one_grad)[0]
        one_sum, one_cross, one_bias = lax.psum(
            (
                jnp.sum(act_one_grad, axis=(0, 1)),
                jnp.sum(act_one_grad * normed_one, axis=(0, 1)),
                jnp.sum(first_low.astype(jnp.float32), axis=(0, 1)),
            ),
            ("batch", "pos"),
        )
        gain_one_grad = gain_one_grad + one_cross
        bias_one_grad = bias_one_grad + one_sum
        conv_one_bias_grad = conv_one_bias_grad + one_bias
        input_step = norm_back(
            act_one_grad, normed_one, inverse_one, norm1_gain, one_sum, one_cross, total_rows
        )
        input_grads.append(input_step.astype(jnp.bfloat16))
        windows = stack_windows(whole_one, local_rows)
        left_one, left_two, left_pool, right_one, right_two, right_pool = (
            lax.all_to_all(windows, "batch", split_axis=2, concat_axis=0, tiled=True),
            lax.all_to_all(whole_two, "batch", split_axis=2, concat_axis=0, tiled=True),
            lax.all_to_all(whole_pool, "batch", split_axis=2, concat_axis=0, tiled=True),
            lax.all_to_all(
                jnp.tile(first_low, (1, 1, pair_count)),
                "batch",
                split_axis=2,
                concat_axis=0,
                tiled=True,
            ),
            lax.all_to_all(
                jnp.tile(branch_grad, (1, 1, pair_count)),
                "batch",
                split_axis=2,
                concat_axis=0,
                tiled=True,
            ),
            lax.all_to_all(
                jnp.tile(logit_low, (1, 1, pair_count)),
                "batch",
                split_axis=2,
                concat_axis=0,
                tiled=True,
            ),
        )
        accum_one = accum_one + weight_product(left_one, right_one)
        accum_two = accum_two + weight_product(left_two, right_two)
        accum_pool = accum_pool + weight_product(left_pool, right_pool)
    shards = (
        lax.psum_scatter(accum_one, "pos", scatter_dimension=0, tiled=True),
        lax.psum_scatter(accum_two, "pos", scatter_dimension=0, tiled=True),
        lax.psum_scatter(accum_pool, "pos", scatter_dimension=0, tiled=True),
    )
    return (
        jnp.stack(outputs),
        jnp.stack(input_grads),
        gain_one_grad,
        bias_one_grad,
        shards[0],
        conv_one_bias_grad,
        gain_two_grad,
        bias_two_grad,
        shards[1],
        conv_two_bias_grad,
        shards[2],
    )


def solution(mesh):
    placed = (
        P(None, "batch", "pos", "ch"),
        P("ch"),
        P("ch"),
        P(None, "ch"),
        P("ch"),
        P("ch"),
        P("ch"),
        P(None, "ch"),
        P("ch"),
        P(None, "ch"),
        P(None, "batch", "pos", "ch"),
        P(),
        P(),
    )
    return jax.shard_map(
        local,
        mesh=mesh,
        in_specs=placed,
        out_specs=(
            P(None, "batch", "pos", "ch"),
            P(None, "batch", "pos", "ch"),
            P("ch"),
            P("ch"),
            P(("batch", "pos"), "ch"),
            P("ch"),
            P("ch"),
            P("ch"),
            P(("batch", "pos"), "ch"),
            P("ch"),
            P(("batch", "pos"), "ch"),
        ),
        check_vma=False,
    )
```

profile of v0, /device:TPU:0, one launch (start us, length us, event | category | flops | bytes accessed | tf_op | source)
XLA Modules:
  0.0 2395.1 jit_solution(102389073933892345)
XLA Ops:
  11.2 35.4 %all-reduce.6 = (f32[640]{0:T(1024)S(1)}, f32[640]{0:T(1024)S(1)}) all-reduce(f32[640]{0:T(1024)S(1)} %fusion.65, f32[640]{0:T(1024)S(1)} %get-tuple-element.28), channel_id=1, replica_groups=mesh['batch'=2,'pos'=8,'ch'=2] {'batch','pos'}, use_global_device_ids=true, to_apply=%region_3.0 | all-reduce | flops 1280 | bytes 10240 | tf_op jit(solution)/shard_map/psum | solution.py:102
  66.1 37.7 %all-gather.11.cloned.1.call-done = bf16[1,1028,1280]{2,1,0:T(8,128)(2,1)} async-done(((bf16[1,1028,640]{2,1,0:T(8,128)(2,1)}), bf16[1,1028,1280]{2,1,0:T(8,128)(2,1)}) %all-gather.11.cloned.1.call-update) | async-done | bytes 2631696 | tf_op jit(solution)/shard_map/all_gather | solution.py:108
  120.9 33.6 %all-reduce.5 = (f32[768]{0:T(1024)S(1)}, f32[768]{0:T(1024)S(1)}) all-reduce(f32[768]{0:T(1024)S(1)} %get-tuple-element.20, f32[768]{0:T(1024)S(1)} %get-tuple-element.19), channel_id=1, replica_groups=mesh['batch'=2,'pos'=8,'ch'=2] {'batch','pos'}, use_global_device_ids=true, to_apply=%region_7.0 | all-reduce | flops 1536 | bytes 12288 | tf_op jit(solution)/shard_map/psum | solution.py:114
  159.3 41.2 %all-gather.15.cloned.1.call-done = bf16[1024,1536]{1,0:T(8,128)(2,1)} async-done(((bf16[1024,768]{1,0:T(8,128)(2,1)}), bf16[1024,1536]{1,0:T(8,128)(2,1)}) %all-gather.15.cloned.1.call-update) | async-done | bytes 3145744 | tf_op jit(solution)/shard_map/all_gather | solution.py:118
  229.5 23.7 all-gather.17.cloned.1.call-done
  340.9 43.5 %reduce-scatter.14.cloned.1.call-done = bf16[1,1024,768]{2,1,0:T(8,128)(2,1)} async-done(((bf16[1,1024,1536]{2,1,0:T(8,128)(2,1)}), bf16[1,1024,768]{2,1,0:T(8,128)(2,1)}) %reduce-scatter.14.cloned.1.call-update) | async-done | bytes 1572880 | tf_op jit(solution)/shard_map/reduce_scatter | solution.py:128
  398.3 43.4 %reduce-scatter.16.cloned.1.call-done = bf16[1,1024,768]{2,1,0:T(8,128)(2,1)} async-done(((bf16[1,1024,1536]{2,1,0:T(8,128)(2,1)}), bf16[1,1024,768]{2,1,0:T(8,128)(2,1)}) %reduce-scatter.16.cloned.1.call-update) | async-done | bytes 1572880 | tf_op jit(solution)/shard_map/reduce_scatter | solution.py:135
  446.2 33.7 %all-reduce.4 = (f32[768]{0:T(1024)S(1)}, f32[768]{0:T(1024)S(1)}) all-reduce(f32[768]{0:T(1024)S(1)} %get-tuple-element.16, f32[768]{0:T(1024)S(1)} %get-tuple-element.15), channel_id=1, replica_groups=mesh['batch'=2,'pos'=8,'ch'=2] {'batch','pos'}, use_global_device_ids=true, to_apply=%region_29.30 | all-reduce | flops 1536 | bytes 12288 | tf_op jit(solution)/shard_map/psum | solution.py:142
  530.4 34.1 %reduce-scatter.28.cloned.1.call-done = bf16[640,1024]{1,0:T(8,128)(2,1)} async-done(((bf16[1280,1024]{1,0:T(8,128)(2,1)}), bf16[640,1024]{1,0:T(8,128)(2,1)}) %reduce-scatter.28.cloned.1.call-update) | async-done | bytes 1310736
  580.6 33.6 %all-reduce.3 = (f32[640]{0:T(1024)S(1)}, f32[640]{0:T(1024)S(1)}) all-reduce(f32[640]{0:T(1024)S(1)} %get-tuple-element.25, f32[640]{0:T(1024)S(1)} %get-tuple-element.29), channel_id=1, replica_groups=mesh['batch'=2,'pos'=8,'ch'=2] {'batch','pos'}, use_global_device_ids=true, to_apply=%region_14.15 | all-reduce | flops 1280 | bytes 10240 | tf_op jit(solution)/shard_map/psum | solution.py:102
  633.3 37.2 %all-gather.13.cloned.1.call-done = bf16[1,1028,1280]{2,1,0:T(8,128)(2,1)} async-done(((bf16[1,1028,640]{2,1,0:T(8,128)(2,1)}), bf16[1,1028,1280]{2,1,0:T(8,128)(2,1)}) %all-gather.13.cloned.1.call-update) | async-done | bytes 2631696 | tf_op jit(solution)/shard_map/all_gather | solution.py:108
  688.1 33.6 %all-reduce.2 = (f32[768]{0:T(1024)S(1)}, f32[768]{0:T(1024)S(1)}) all-reduce(f32[768]{0:T(1024)S(1)} %get-tuple-element.22, f32[768]{0:T(1024)S(1)} %get-tuple-element.21), channel_id=1, replica_groups=mesh['batch'=2,'pos'=8,'ch'=2] {'batch','pos'}, use_global_device_ids=true, to_apply=%region_18.19 | all-reduce | flops 1536 | bytes 12288 | tf_op jit(solution)/shard_map/psum | solution.py:114
  727.4 41.4 %all-gather.19.cloned.1.call-done = bf16[1024,1536]{1,0:T(8,128)(2,1)} async-done(((bf16[1024,768]{1,0:T(8,128)(2,1)}), bf16[1024,1536]{1,0:T(8,128)(2,1)}) %all-gather.19.cloned.1.call-update) | async-done | bytes 3145744 | tf_op jit(solution)/shard_map/all_gather | solution.py:118
  795.4 26.2 %all-gather.21.cloned.1.call-done = bf16[1024,1536]{1,0:T(8,128)(2,1)} async-done(((bf16[1024,768]{1,0:T(8,128)(2,1)}), bf16[1024,1536]{1,0:T(8,128)(2,1)}) %all-gather.21.cloned.1.call-update) | async-done | bytes 3145744 | tf_op jit(solution)/shard_map/all_gather | solution.py:120
  967.4 53.0 %copy.66 = bf16[1,1024,6400]{1,0,2:T(2,128)(2,1)} copy(bf16[1,1024,6400]{2,1,0:T(8,128)(2,1)} %slice_dynamic-update-slice_fusion.5) | data formatting | bytes 26214400 | tf_op jit(solution)/shard_map/concatenate | solution.py:60
  1020.4 76.0 %reduce.18 = bf16[6400,1024]{1,0:T(8,128)(2,1)} reduce(bf16[6400,1,1024]{2,1,0:T(2,128)(2,1)} %bitcast.508, bf16[]{:T(256)} %broadcast.1731), dimensions={1}, to_apply=%bitcast.430.reduce_sub_computation | reduce | bytes 26214402
  1096.4 20.6 reshape.1955
  1144.5 21.6 copy.119
  1190.9 77.7 %all-to-all-done = bf16[2,2,1638400]{2,1,0:T(2,128)(2,1)} async-done(((bf16[2,2,1638400]{2,1,0:T(2,128)(2,1)}), bf16[2,2,1638400]{2,1,0:T(2,128)(2,1)}, u32[]{:S(2)}, u32[]{:S(2)}) %all-to-all-start) | async-done | bytes 13107232 | tf_op jit(solution)/shard_map/all_to_all | solution.py:187
  1323.4 21.6 copy.121
  1378.6 21.6 copy.123
  1474.8 21.6 copy.118
  1566.2 33.2 %all-reduce.1 = (f32[768]{0:T(1024)S(1)}, f32[768]{0:T(1024)S(1)}) all-reduce(f32[768]{0:T(1024)S(1)} %get-tuple-element.18, f32[768]{0:T(1024)S(1)} %get-tuple-element.17), channel_id=1, replica_groups=mesh['batch'=2,'pos'=8,'ch'=2] {'batch','pos'}, use_global_device_ids=true, to_apply=%region_42.43 | all-reduce | flops 1536 | bytes 12288 | tf_op jit(solution)/shard_map/psum | solution.py:142
  1613.1 25.3 %all-to-all-done.6 = bf16[2,2,393216]{2,1,0:T(2,128)(2,1)} async-done(((bf16[2,2,393216]{2,1,0:T(2,128)(2,1)}), bf16[2,2,393216]{2,1,0:T(2,128)(2,1)}, u32[]{:S(2)}, u32[]{:S(2)}) %all-to-all-start.6) | async-done | bytes 3145760 | tf_op jit(solution)/shard_map/all_to_all | solution.py:188
  1718.2 21.6 copy.120
  1778.4 53.0 %copy.70 = bf16[1,1024,6400]{1,0,2:T(2,128)(2,1)} copy(bf16[1,1024,6400]{2,1,0:T(8,128)(2,1)} %slice_dynamic-update-slice_fusion) | data formatting | bytes 26214400 | tf_op jit(solution)/shard_map/concatenate | solution.py:60
  1831.5 76.1 %reduce.20 = bf16[6400,1024]{1,0:T(8,128)(2,1)} reduce(bf16[6400,1,1024]{2,1,0:T(2,128)(2,1)} %bitcast.509, bf16[]{:T(256)} %broadcast.1731), dimensions={1}, to_apply=%bitcast.434.reduce_sub_computation | reduce | bytes 26214402
  1907.5 20.6 reshape.1959
  2063.4 30.9 %reshape.1956 = bf16[6400,1,1024]{2,1,0:T(2,128)(2,1)} reshape(bf16[2,2,1638400]{2,1,0:T(2,128)(2,1)} %all-to-all-done) | data formatting | bytes 26214400
  2131.6 21.6 copy.122
  2200.2 30.8 %reshape.1960 = bf16[6400,1,1024]{2,1,0:T(2,128)(2,1)} reshape(bf16[2,2,1638400]{2,1,0:T(2,128)(2,1)} %all-to-all-done.2) | data formatting | bytes 26214400
  2299.2 66.2 %all-reduce = (f32[640]{0:T(1024)S(1)}, f32[640]{0:T(1024)S(1)}, f32[640]{0:T(1024)S(1)}, f32[640]{0:T(1024)S(1)}, f32[768]{0:T(1024)}, /*index=5*/f32[768]{0:T(1024)}) all-reduce(f32[640]{0:T(1024)S(1)} %get-tuple-element.27, f32[640]{0:T(1024)S(1)} %get-tuple-element.26, ...), channel_id=1, replica_groups=mesh['batch'=2,'pos'=8,'ch'=2] {'batch','pos'}, use_global_device_ids=true, to_apply=%region_47.48 | all-reduce | flops 4096 | bytes 32768 | tf_op jit(solution)/shard_map/psum | solution.py:170
  (424 shorter events, 1188.3 us)
Async XLA Ops:
  7.2 96.6 %all-gather.11.cloned.1.call-start = ((), (), s32[]{:S(2)}) async-start(), calls=%async_computation.21 | async-start | bytes 3962880 | tf_op jit(solution)/shard_map/all_gather | solution.py:108
  65.6 134.9 %all-gather.15.cloned.1.call-start = ((), (), s32[]{:S(2)}) async-start(), calls=%async_computation.30 | async-start | bytes 4718592 | tf_op jit(solution)/shard_map/all_gather | solution.py:118
  159.1 94.2 %all-gather.17.cloned.1.call-start = ((), (), s32[]{:S(2)}) async-start(), calls=%async_computation.31 | async-start | bytes 4718592 | tf_op jit(solution)/shard_map/all_gather | solution.py:120
  208.1 176.2 %reduce-scatter.14.cloned.1.call-start = ((), (), s32[]{:S(2)}) async-start(), calls=%async_computation.23 | async-start | bytes 4718592 | tf_op jit(solution)/shard_map/reduce_scatter | solution.py:128
  340.9 100.8 %reduce-scatter.16.cloned.1.call-start = ((), (), s32[]{:S(2)}) async-start(), calls=%async_computation.24 | async-start | bytes 4718592 | tf_op jit(solution)/shard_map/reduce_scatter | solution.py:135
  398.2 166.2 %reduce-scatter.28.cloned.1.call-start = ((), (), s32[]{:S(2)}) async-start(), calls=%async_computation.34 | async-start | bytes 3932160
  486.1 8.8 collective-permute-start.4
  491.5 10.4 collective-permute-start.5
  530.4 140.2 %all-gather.13.cloned.1.call-start = ((), (), s32[]{:S(2)}) async-start(), calls=%async_computation.22 | async-start | bytes 3962880 | tf_op jit(solution)/shard_map/all_gather | solution.py:108
  618.6 4.5 collective-permute-start.3
  633.3 135.5 %all-gather.19.cloned.1.call-start = ((), (), s32[]{:S(2)}) async-start(), calls=%async_computation.32 | async-start | bytes 4718592 | tf_op jit(solution)/shard_map/all_gather | solution.py:118
  727.4 94.2 %all-gather.21.cloned.1.call-start = ((), (), s32[]{:S(2)}) async-start(), calls=%async_computation.33 | async-start | bytes 4718592 | tf_op jit(solution)/shard_map/all_gather | solution.py:120
  776.5 349.1 %reduce-scatter.18.cloned.1.call-start = ((), (), s32[]{:S(2)}) async-start(), calls=%async_computation.25 | async-start | bytes 4718592 | tf_op jit(solution)/shard_map/reduce_scatter | solution.py:128
  953.7 163.2 %all-to-all-start.4 = ((bf16[2,2,393216]{2,1,0:T(2,128)(2,1)}), bf16[2,2,393216]{2,1,0:T(2,128)(2,1)}, u32[]{:S(2)}, u32[]{:S(2)}) async-start(bf16[2,2,393216]{2,1,0:T(2,128)(2,1)} %reshape.1967), calls=%async_computation.9 | async-start | bytes 6291456 | tf_op jit(solution)/shard_map/all_to_all | solution.py:188
  1117.0 151.7 %all-to-all-start = ((bf16[2,2,1638400]{2,1,0:T(2,128)(2,1)}), bf16[2,2,1638400]{2,1,0:T(2,128)(2,1)}, u32[]{:S(2)}, u32[]{:S(2)}) async-start(bf16[2,2,1638400]{2,1,0:T(2,128)(2,1)} %reshape.1955), calls=%async_computation.4 | async-start | bytes 26214400 | tf_op jit(solution)/shard_map/all_to_all | solution.py:187
  1125.5 436.2 %reduce-scatter.20.cloned.1.call-start = ((), (), s32[]{:S(2)}) async-start(), calls=%async_computation.26 | async-start | bytes 4718592 | tf_op jit(solution)/shard_map/reduce_scatter | solution.py:135
  1268.6 45.7 %all-to-all-start.9 = ((bf16[2,2,393216]{2,1,0:T(2,128)(2,1)}), bf16[2,2,393216]{2,1,0:T(2,128)(2,1)}, u32[]{:S(2)}, u32[]{:S(2)}) async-start(bf16[2,2,393216]{2,1,0:T(2,128)(2,1)} %reshape.1977), calls=%async_computation.15 | async-start | bytes 6291456 | tf_op jit(solution)/shard_map/all_to_all | solution.py:204
  1314.4 55.4 %all-to-all-start.8 = ((bf16[2,2,393216]{2,1,0:T(2,128)(2,1)}), bf16[2,2,393216]{2,1,0:T(2,128)(2,1)}, u32[]{:S(2)}, u32[]{:S(2)}) async-start(bf16[2,2,393216]{2,1,0:T(2,128)(2,1)} %reshape.1975), calls=%async_computation.14 | async-start | bytes 6291456 | tf_op jit(solution)/shard_map/all_to_all | solution.py:189
  1369.8 55.3 %all-to-all-start.5 = ((bf16[2,2,393216]{2,1,0:T(2,128)(2,1)}), bf16[2,2,393216]{2,1,0:T(2,128)(2,1)}, u32[]{:S(2)}, u32[]{:S(2)}) async-start(bf16[2,2,393216]{2,1,0:T(2,128)(2,1)} %reshape.1969), calls=%async_computation.10 | async-start | bytes 6291456 | tf_op jit(solution)/shard_map/all_to_all | solution.py:197
  1425.1 174.3 %all-to-all-start.1 = ((bf16[2,2,393216]{2,1,0:T(2,128)(2,1)}), bf16[2,2,393216]{2,1,0:T(2,128)(2,1)}, u32[]{:S(2)}, u32[]{:S(2)}) async-start(bf16[2,2,393216]{2,1,0:T(2,128)(2,1)} %reshape.1957), calls=%async_computation.5 | async-start | bytes 6291456 | tf_op jit(solution)/shard_map/all_to_all | solution.py:190
  1599.4 39.0 %all-to-all-start.6 = ((bf16[2,2,393216]{2,1,0:T(2,128)(2,1)}), bf16[2,2,393216]{2,1,0:T(2,128)(2,1)}, u32[]{:S(2)}, u32[]{:S(2)}) async-start(bf16[2,2,393216]{2,1,0:T(2,128)(2,1)} %reshape.1963), calls=%async_computation.11 | async-start | bytes 6291456 | tf_op jit(solution)/shard_map/all_to_all | solution.py:188
  1611.8 39.2 %collective-permute-start.6 = (bf16[1,2,768]{2,1,0:T(2,128)(2,1)S(1)}, bf16[1,2,768]{2,1,0:T(2,128)(2,1)S(1)}, u32[]{:S(2)}, u32[]{:S(2)}) collective-permute-start(bf16[1,2,768]{2,1,0:T(2,128)(2,1)S(1)} %get-tuple-element.62), channel_id=1, source_target_pairs={{2,0},{4,2},{6,4},{8,6},{10,8},{12,10},{14,12},{3,1},{5,3},{7,5},{... | collective-permute-start | bytes 9224 | tf_op jit(solution)/shard_map/ppermute | solution.py:20
  1638.4 38.1 %all-to-all-start.11 = ((bf16[2,2,393216]{2,1,0:T(2,128)(2,1)}), bf16[2,2,393216]{2,1,0:T(2,128)(2,1)}, u32[]{:S(2)}, u32[]{:S(2)}) async-start(bf16[2,2,393216]{2,1,0:T(2,128)(2,1)} %reshape.1973), calls=%async_computation.17 | async-start | bytes 6291456 | tf_op jit(solution)/shard_map/all_to_all | solution.py:204
  1649.8 13.5 collective-permute-start.7
  1676.5 88.2 %all-to-all-start.10 = ((bf16[2,2,393216]{2,1,0:T(2,128)(2,1)}), bf16[2,2,393216]{2,1,0:T(2,128)(2,1)}, u32[]{:S(2)}, u32[]{:S(2)}) async-start(bf16[2,2,393216]{2,1,0:T(2,128)(2,1)} %reshape.1971), calls=%async_computation.16 | async-start | bytes 6291456 | tf_op jit(solution)/shard_map/all_to_all | solution.py:189
  1681.7 603.5 %reduce-scatter.30.cloned.1.call-start = ((), (), s32[]{:S(2)}) async-start(), calls=%async_computation.35 | async-start | bytes 3932160
  1764.7 163.4 %all-to-all-start.7 = ((bf16[2,2,393216]{2,1,0:T(2,128)(2,1)}), bf16[2,2,393216]{2,1,0:T(2,128)(2,1)}, u32[]{:S(2)}, u32[]{:S(2)}) async-start(bf16[2,2,393216]{2,1,0:T(2,128)(2,1)} %reshape.1965), calls=%async_computation.12 | async-start | bytes 6291456 | tf_op jit(solution)/shard_map/all_to_all | solution.py:197
  1928.1 249.9 %all-to-all-start.2 = ((bf16[2,2,1638400]{2,1,0:T(2,128)(2,1)}), bf16[2,2,1638400]{2,1,0:T(2,128)(2,1)}, u32[]{:S(2)}, u32[]{:S(2)}) async-start(bf16[2,2,1638400]{2,1,0:T(2,128)(2,1)} %reshape.1959), calls=%async_computation.6 | async-start | bytes 26214400 | tf_op jit(solution)/shard_map/all_to_all | solution.py:187
  1936.6 436.7 %reduce-scatter.26.cloned.1.call-start = ((), (), s32[]{:S(2)}) async-start(), calls=%async_computation.29 | async-start | bytes 2654208 | tf_op jit(solution)/shard_map/reduce_scatter | solution.py:218
  1997.7 375.6 %reduce-scatter.24.cloned.1.call-start = ((), (), s32[]{:S(2)}) async-start(), calls=%async_computation.28 | async-start | bytes 2654208 | tf_op jit(solution)/shard_map/reduce_scatter | solution.py:217
  2178.0 70.3 %all-to-all-start.3 = ((bf16[2,2,393216]{2,1,0:T(2,128)(2,1)}), bf16[2,2,393216]{2,1,0:T(2,128)(2,1)}, u32[]{:S(2)}, u32[]{:S(2)}) async-start(bf16[2,2,393216]{2,1,0:T(2,128)(2,1)} %reshape.1961), calls=%async_computation.7 | async-start | bytes 6291456 | tf_op jit(solution)/shard_map/all_to_all | solution.py:190
  2183.2 205.2 %reduce-scatter.22.cloned.1.call-start = ((), (), s32[]{:S(2)}) async-start(), calls=%async_computation.27 | async-start | bytes 11059200 | tf_op jit(solution)/shard_map/reduce_scatter | solution.py:216
  (82 other events, 2246.4 us)
Sparse Core Ops, SparseCore 0:
  65.7 38.0 all-gather.10
  159.2 41.2 all-gather.14
  208.3 44.9 all-gather.16
  341.0 43.3 reduce-scatter.13
  398.3 43.3 reduce-scatter.15
  530.5 33.9 reduce-scatter.27
  633.4 37.1 all-gather.12
  727.5 41.2 all-gather.18
  776.6 44.9 all-gather.20
  909.0 43.3 reduce-scatter.17
  1139.8 43.8 reduce-scatter.19
  1708.7 38.7 reduce-scatter.29
  1997.8 37.5 reduce-scatter.25
  2063.5 37.6 reduce-scatter.23
  2282.7 105.7 reduce-scatter.21
where the time goes:
time: 2410 us; the launch traced here: 2400 us
  local copies, waits for them, and re-layouts  869 us (36%)
  other arithmetic  511 us (21%)
  waiting for transfers between devices  455 us (19%)
  blocking collectives  269 us (11%)
  matrix products  187 us (8%)
  starting transfers between devices  87.1 us (4%)
    unnamed x211, local copies, waits for them, and re-layouts  396 us
    unnamed x14, other arithmetic  351 us
    concatenate x4, local copies, waits for them, and re-layouts, stack_windows(): jnp.concatenate([whole_one[:, offset:offset + local_rows] for offset in r...  110 us
    all_gather x2, waiting for transfers between devices, local(): lax.all_gather(gelu_two.astype(jnp.bfloat16), 'ch', axis=2, tiled=True)  82.6 us
    all_to_all x2, waiting for transfers between devices, local(): lax.all_to_all(windows, 'batch', split_axis=2, concat_axis=0, tiled=True)  77.7 us
    all_gather x2, waiting for transfers between devices, local(): whole_one = lax.all_gather(rim_one, 'ch', axis=2, tiled=True)  74.9 us
    dot_general x14, matrix products, back_product(): jnp.einsum('slo,co->slc', left, right, preferred_element_type=jnp.float32)  73.9 us
    psum x2, blocking collectives, local(): sums_one = lax.psum(moments(inputs), ('batch', 'pos'))  69 us
  transfers between devices with their start and end apart: 35, of which 15 were waited for; matrix products, arithmetic and copies ran while one was open for 51% of the time, Pallas kernels for 0%

commit v1 on v0

v1 whole, which is shorter than its diff:
```python
import functools

import jax
import jax.numpy as jnp
from jax import lax
from jax.experimental import pallas as pl
from jax.experimental.pallas import tpu as pltpu
from jax.sharding import PartitionSpec as P

KW = 5
RIM = KW // 2
PIECES = KW + 1
EPS = 1e-05
MESH = pl.DeviceIdType.MESH
C0 = 0.7978845608028654
C1 = 0.044715
F32 = jnp.float32
BF16 = jnp.bfloat16
VMEM_LIMIT = 60 * 1024 * 1024

NT = (((1,), (1,)), ((), ()))
TN = (((0,), (0,)), ((), ()))


def params(**kw):
    return pltpu.CompilerParams(vmem_limit_bytes=VMEM_LIMIT, **kw)


def gelu(u):
    return 0.5 * u * (1.0 + jnp.tanh(C0 * (u + C1 * u * u * u)))


def gelu_slope(u):
    square = u * u
    t = jnp.tanh(C0 * (u + C1 * square * u))
    return 0.5 * (1.0 + t) + 0.5 * u * (1.0 - t * t) * (C0 + (3.0 * C0 * C1) * square)


def reduce_kernel(v_ref, o_ref, near, mid, far, near_send, near_recv, far_send, far_recv):
    batch, pos, ch = (lax.axis_index(a) for a in ("batch", "pos", "ch"))
    pos_count = lax.axis_size("pos")
    me = batch * 2 + ch
    barrier = pltpu.get_barrier_semaphore()
    peers = []
    for step in range(1, 4):
        other = lax.rem(me + step, 4)
        peers.append((other // 2, pos, lax.rem(other, 2)))
    for step in range(1, pos_count):
        peers.append((batch, lax.rem(pos + step, pos_count), ch))
    for peer in peers:
        pl.semaphore_signal(barrier, inc=1, device_id=peer, device_id_type=MESH)
    near[pl.ds(me, 1)] = v_ref[...][None]
    pl.semaphore_wait(barrier, len(peers))
    copies = [
        pltpu.make_async_remote_copy(
            v_ref, near.at[me], near_send.at[i], near_recv.at[i], device_id=peer, device_id_type=MESH
        )
        for i, peer in enumerate(peers[:3])
    ]
    for copy in copies:
        copy.start()
    for copy in copies:
        copy.wait()
    mid[...] = (near[0] + near[1]) + (near[2] + near[3])
    far[pl.ds(pos, 1)] = mid[...][None]
    copies = [
        pltpu.make_async_remote_copy(
            mid, far.at[pos], far_send.at[i], far_recv.at[i], device_id=peer, device_id_type=MESH
        )
        for i, peer in enumerate(peers[3:])
    ]
    for copy in copies:
        copy.start()
    for copy in copies:
        copy.wait()
    total = far[0]
    for i in range(1, pos_count):
        total = total + far[i]
    o_ref[...] = total


def reduce_all(values, collective_id):
    rows, width = values.shape
    padded = -(-rows // 8) * 8
    values = jnp.pad(values, ((0, padded - rows), (0, 0)))
    pos_count = lax.axis_size("pos")
    shape = (padded, width)
    total = pl.pallas_call(
        reduce_kernel,
        out_shape=jax.ShapeDtypeStruct(shape, F32),
        in_specs=[pl.BlockSpec(memory_space=pltpu.VMEM)],
        out_specs=pl.BlockSpec(memory_space=pltpu.VMEM),
        scratch_shapes=[
            pltpu.VMEM((4,) + shape, F32),
            pltpu.VMEM(shape, F32),
            pltpu.VMEM((pos_count,) + shape, F32),
            pltpu.SemaphoreType.DMA((3,)),
            pltpu.SemaphoreType.DMA((3,)),
            pltpu.SemaphoreType.DMA((pos_count - 1,)),
            pltpu.SemaphoreType.DMA((pos_count - 1,)),
        ],
        compiler_params=params(collective_id=collective_id, has_side_effects=True),
    )(values)
    return total[:rows]


def hidden_kernel(who, x_ref, vec_ref, h_ref, x_out, scr, raw):
    micro, order = pl.program_id(0), pl.program_id(1)
    half = h_ref.shape[3] * 2
    lanes, ext = scr.shape[:2]
    side = jnp.bitwise_xor(who[0], order)
    begin = pl.multiple_of(side * half, 16)
    first = who[1] + side * half - RIM
    total = who[2]
    center = vec_ref[0, 0:1, :]
    scale = vec_ref[0, 1:2, :]
    bias = vec_ref[0, 2:3, :]

    @pl.loop(0, ext // 16)
    def _(i):
        at = pl.multiple_of(i * 16, 16)
        x = x_ref[0, pl.ds(begin + at, 16), :].astype(F32)
        act = (x - center) * scale + bias
        row = first + at + lax.broadcasted_iota(jnp.int32, x.shape, 0)
        inside = jnp.logical_and(row >= 0, row < total)
        hidden = jnp.where(inside, gelu(act), 0.0)
        for b in range(lanes):
            scr[b, pl.ds(at, 16), :] = hidden[:, b * 128 : (b + 1) * 128]
            raw[b, pl.ds(at, 16), :] = x[:, b * 128 : (b + 1) * 128]

    pairs = half // 2

    @pl.loop(0, pairs // 16)
    def _(i):
        at = pl.multiple_of(i * 16, 16)
        for b in range(lanes):
            lane = slice(b * 128, (b + 1) * 128)
            for d in range(PIECES):
                h_ref[0, d, 0, pl.ds(at, 16), lane] = scr[b, pl.ds(d + 2 * at, 16, stride=2), :].astype(BF16)
            for e in range(2):
                x_out[0, e, 0, pl.ds(at, 16), lane] = raw[
                    b, pl.ds(RIM + e + 2 * at, 16, stride=2), :
                ].astype(BF16)


def make_hidden(who, x_ext, vecs, half):
    micro_count, rows, wide = x_ext.shape
    ext = half + 16
    pairs = half // 2
    return pl.pallas_call(
        hidden_kernel,
        out_shape=(
            jax.ShapeDtypeStruct((2, PIECES, micro_count, pairs, wide), BF16),
            jax.ShapeDtypeStruct((2, 2, micro_count, pairs, wide), BF16),
        ),
        grid_spec=pltpu.PrefetchScalarGridSpec(
            num_scalar_prefetch=1,
            grid=(micro_count, 2),
            in_specs=[
                pl.BlockSpec((1, rows, wide), lambda m, o, w: (m, 0, 0)),
                pl.BlockSpec((1, 8, wide), lambda m, o, w: (m, 0, 0)),
            ],
            out_specs=(
                pl.BlockSpec((1, PIECES, 1, pairs, wide), lambda m, o, w: (o, 0, m, 0, 0)),
                pl.BlockSpec((1, 2, 1, pairs, wide), lambda m, o, w: (o, 0, m, 0, 0)),
            ),
            scratch_shapes=[pltpu.VMEM((wide // 128, ext, 128), F32)] * 2,
        ),
        compiler_params=params(),
        name="hidden",
    )(who, x_ext, vecs)


def conv_kernel(h_ref, w_ref, b_ref, o_ref, s_ref):
    micro_count, pairs = o_ref.shape[1:3]
    rows = micro_count * pairs
    wide = h_ref.shape[2]
    sums = [[0.0, 0.0] for _ in range(micro_count)]
    for e in range(2):
        acc = jnp.dot(h_ref[e], w_ref[0:wide, :], preferred_element_type=F32)
        for k in range(1, KW):
            acc += jnp.dot(
                h_ref[k + e], w_ref[k * wide : (k + 1) * wide, :], preferred_element_type=F32
            )
        acc += b_ref[...]
        for m in range(micro_count):
            part = acc[m * pairs : (m + 1) * pairs]
            o_ref[e, m] = part
            sums[m][0] += jnp.sum(part, axis=0, keepdims=True)
            sums[m][1] += jnp.sum(part * part, axis=0, keepdims=True)
    for m in range(micro_count):
        for i in range(2):
            s_ref[2 * m + i : 2 * m + i + 1, :] = sums[m][i]


def conv_forward(pieces, weight, bias, tile=256):
    _, micro_count, pairs, wide = pieces.shape
    out = weight.shape[1]
    rows = micro_count * pairs
    return pl.pallas_call(
        conv_kernel,
        out_shape=(
            jax.ShapeDtypeStruct((2, micro_count, pairs, out), F32),
            jax.ShapeDtypeStruct((8, out), F32),
        ),
        grid=(out // tile,),
        in_specs=[
            pl.BlockSpec((PIECES, rows, wide), lambda j: (0, 0, 0)),
            pl.BlockSpec((KW * wide, tile), lambda j: (0, j)),
            pl.BlockSpec((1, tile), lambda j: (0, j)),
        ],
        out_specs=(
            pl.BlockSpec((2, micro_count, pairs, tile), lambda j: (0, 0, 0, j)),
            pl.BlockSpec((8, tile), lambda j: (0, j)),
        ),
        compiler_params=params(),
        name="conv_forward",
    )(pieces.reshape(PIECES, rows, wide), weight, bias.reshape(1, out))


def middle_kernel(
    fo_ref,
    fx_ref,
    vec_ref,
    w2_ref,
    wp_ref,
    og_ref,
    lim_ref,
    pooled_ref,
    hid_ref,
    branch_ref,
    diff_ref,
    lg_ref,
    a2g_ref,
    sg_ref,
    sum_ref,
    so,
):
    pairs = og_ref.shape[2]
    rows = 2 * pairs
    wide = w2_ref.shape[0]
    half = wide // 2
    tile = 256
    tiles = wide // tile

    def columns(j):
        return pl.ds(pl.multiple_of(j * tile, tile), tile)

    def load_first(j, e):
        own = j < tiles // 2
        at = pl.ds(pl.multiple_of(lax.rem(j, tiles // 2) * tile, tile), tile)
        return jnp.where(own, fo_ref[e, 0, :, at], fx_ref[e, 0, :, at])

    @pl.loop(0, tiles)
    def _(j):
        c = columns(j)
        for e in range(2):
            f = load_first(j, e)
            act = (f - vec_ref[0, 0:1, c]) * vec_ref[0, 1:2, c] * vec_ref[0, 2:3, c] + vec_ref[0, 3:4, c]
            hid_ref[0, pl.ds(e * pairs, pairs), c] = gelu(act).astype(BF16)

    @pl.loop(0, tiles)
    def _(j):
        c = columns(j)
        branch = jnp.dot(hid_ref[0], w2_ref[:, c], preferred_element_type=F32)
        even = branch[:pairs] + (load_first(j, 0) + vec_ref[0, 4:5, c])
        odd = branch[pairs:] + (load_first(j, 1) + vec_ref[0, 4:5, c])
        so[0, :, c] = even
        so[1, :, c] = odd
        diff_ref[0, :, c] = (even - odd).astype(BF16)

    limit = lim_ref[0, 0:1, 0:1]
    inverse_limit = 1.0 / limit

    @pl.loop(0, tiles)
    def _(j):
        c = columns(j)
        d = jnp.dot(diff_ref[0], wp_ref[:, c], preferred_element_type=F32)
        t = jnp.tanh(0.5 * d)
        weight_even = 0.5 + 0.5 * t
        weight_odd = 0.5 - 0.5 * t
        even, odd = so[0, :, c], so[1, :, c]
        pooled_ref[0, :, c] = (weight_even * even + weight_odd * odd).astype(BF16)
        clipped = limit * jnp.tanh(og_ref[0, 0, :, c].astype(F32) * inverse_limit)
        lg_ref[0, :, c] = (weight_even * weight_odd * (even - odd) * clipped).astype(BF16)
        sg_ref[0, 0, :, c] = weight_even * clipped
        sg_ref[1, 0, :, c] = weight_odd * clipped

    @pl.loop(0, tiles)
    def _(j):
        c = columns(j)
        g = lax.dot_general(lg_ref[0], wp_ref[c, :], NT, preferred_element_type=F32)
        even = sg_ref[0, 0, :, c] + g
        odd = sg_ref[1, 0, :, c] - g
        sg_ref[0, 0, :, c] = even
        sg_ref[1, 0, :, c] = odd
        low_even, low_odd = even.astype(BF16), odd.astype(BF16)
        branch_ref[0, pl.ds(0, pairs), c] = low_even
        branch_ref[0, pl.ds(pairs, pairs), c] = low_odd
        sum_ref[0, 2:3, c] = jnp.sum(low_even.astype(F32) + low_odd.astype(F32), axis=0, keepdims=True)

    @pl.loop(0, tiles)
    def _(j):
        c = columns(j)
        hg = lax.dot_general(branch_ref[0], w2_ref[c, :], NT, preferred_element_type=F32)
        plain, cross = 0.0, 0.0
        for e in range(2):
            f = load_first(j, e)
            normed = (f - vec_ref[0, 0:1, c]) * vec_ref[0, 1:2, c]
            act = normed * vec_ref[0, 2:3, c] + vec_ref[0, 3:4, c]
            grad = hg[e * pairs : (e + 1) * pairs] * gelu_slope(act)
            a2g_ref[e, 0, :, c] = grad
            plain += jnp.sum(grad, axis=0, keepdims=True)
            cross += jnp.sum(grad * normed, axis=0, keepdims=True)
        sum_ref[0, 0:1, c] = plain
        sum_ref[0, 1:2, c] = cross


def middle(first_own, first_other, vecs, w2, wp, out_grad, limits):
    _, micro_count, pairs, half = first_own.shape
    wide = 2 * half
    rows = 2 * pairs
    return pl.pallas_call(
        middle_kernel,
        out_shape=(
            jax.ShapeDtypeStruct((micro_count, pairs, wide), BF16),
            jax.ShapeDtypeStruct((micro_count, rows, wide), BF16),
            jax.ShapeDtypeStruct((micro_count, rows, wide), BF16),
            jax.ShapeDtypeStruct((micro_count, pairs, wide), BF16),
            jax.ShapeDtypeStruct((micro_count, pairs, wide), BF16),
            jax.ShapeDtypeStruct((2, micro_count, pairs, wide), F32),
            jax.ShapeDtypeStruct((2, micro_count, pairs, wide), F32),
            jax.ShapeDtypeStruct((micro_count, 8, wide), F32),
        ),
        grid=(micro_count,),
        in_specs=[
            pl.BlockSpec((2, 1, pairs, half), lambda m: (0, m, 0, 0)),
            pl.BlockSpec((2, 1, pairs, half), lambda m: (0, m, 0, 0)),
            pl.BlockSpec((1, 8, wide), lambda m: (m, 0, 0)),
            pl.BlockSpec((wide, wide), lambda m: (0, 0), pipeline_mode=pl.Buffered(1)),
            pl.BlockSpec((wide, wide), lambda m: (0, 0), pipeline_mode=pl.Buffered(1)),
            pl.BlockSpec((1, 1, pairs, wide), lambda m: (m, 0, 0, 0)),
            pl.BlockSpec((1, 8, 128), lambda m: (m, 0, 0)),
        ],
        out_specs=(
            pl.BlockSpec((1, pairs, wide), lambda m: (m, 0, 0)),
            pl.BlockSpec((1, rows, wide), lambda m: (m, 0, 0)),
            pl.BlockSpec((1, rows, wide), lambda m: (m, 0, 0)),
            pl.BlockSpec((1, pairs, wide), lambda m: (m, 0, 0)),
            pl.BlockSpec((1, pairs, wide), lambda m: (m, 0, 0)),
            pl.BlockSpec((2, 1, pairs, wide), lambda m: (0, m, 0, 0)),
            pl.BlockSpec((2, 1, pairs, wide), lambda m: (0, m, 0, 0)),
            pl.BlockSpec((1, 8, wide), lambda m: (m, 0, 0)),
        ),
        scratch_shapes=[pltpu.VMEM((2, pairs, wide), F32)],
        compiler_params=params(),
        name="middle",
    )(first_own, first_other, vecs, w2, wp, out_grad, limits)


def back_kernel(g_ref, wo_ref, wx_ref, x_ref, vec_ref, o_ref, s_ref):
    micro_count, pairs = o_ref.shape[1:3]
    half = wo_ref.shape[2]
    sums = [[0.0, 0.0] for _ in range(micro_count)]
    for e in range(2):
        acc = 0.0
        for k in range(KW):
            d = e - k + KW - 1
            acc += lax.dot_general(g_ref[d, :, :half], wo_ref[k], NT, preferred_element_type=F32)
            acc += lax.dot_general(g_ref[d, :, half:], wx_ref[k], NT, preferred_element_type=F32)
        for m in range(micro_count):
            x = x_ref[e, m].astype(F32)
            normed = (x - vec_ref[m, 0:1, :]) * vec_ref[m, 3:4, :]
            act = (x - vec_ref[m, 0:1, :]) * vec_ref[m, 1:2, :] + vec_ref[m, 2:3, :]
            grad = acc[m * pairs : (m + 1) * pairs] * gelu_slope(act)
            o_ref[e, m] = grad
            sums[m][0] += jnp.sum(grad, axis=0, keepdims=True)
            sums[m][1] += jnp.sum(grad * normed, axis=0, keepdims=True)
    for m in range(micro_count):
        for i in range(2):
            s_ref[2 * m + i : 2 * m + i + 1, :] = sums[m][i]


def conv_back(pieces, own, other, x, vecs, tile=256):
    _, micro_count, pairs, out = pieces.shape
    wide = own.shape[0] // KW
    half = own.shape[1]
    rows = micro_count * pairs
    return pl.pallas_call(
        back_kernel,
        out_shape=(
            jax.ShapeDtypeStruct((2, micro_count, pairs, wide), F32),
            jax.ShapeDtypeStruct((8, wide), F32),
        ),
        grid=(wide // tile,),
        in_specs=[
            pl.BlockSpec((PIECES, rows, out), lambda j: (0, 0, 0)),
            pl.BlockSpec((KW, tile, half), lambda j: (0, j, 0)),
            pl.BlockSpec((KW, tile, half), lambda j: (0, j, 0)),
            pl.BlockSpec((2, micro_count, pairs, tile), lambda j: (0, 0, 0, j)),
            pl.BlockSpec((micro_count, 8, tile), lambda j: (0, 0, j)),
        ],
        out_specs=(
            pl.BlockSpec((2, micro_count, pairs, tile), lambda j: (0, 0, 0, j)),
            pl.BlockSpec((8, tile), lambda j: (0, j)),
        ),
        compiler_params=params(),
        name="conv_back",
    )(
        pieces.reshape(PIECES, rows, out),
        own.reshape(KW, wide, half),
        other.reshape(KW, wide, half),
        x,
        vecs,
    )


def weight_kernel(he_ref, ho_ref, f_ref, o_ref):
    acc = 0.0
    for s in range(f_ref.shape[0]):
        acc += lax.dot_general(he_ref[s, 0], f_ref[s, 0], TN, preferred_element_type=F32)
        acc += lax.dot_general(ho_ref[s, 0], f_ref[s, 1], TN, preferred_element_type=F32)
    o_ref[...] = acc.astype(BF16)


def conv_weight_grad(pieces, low, tile=256):
    sides, _, micro_count, pairs, wide = pieces.shape
    out = low.shape[-1]
    rows = micro_count * pairs
    pieces = pieces.reshape(sides, PIECES, rows, wide)
    low = low.reshape(sides, 2, rows, out)
    per = wide // tile
    return pl.pallas_call(
        weight_kernel,
        out_shape=jax.ShapeDtypeStruct((KW * wide, out), BF16),
        grid=(KW, per),
        in_specs=[
            pl.BlockSpec((sides, 1, rows, tile), lambda k, j: (0, k, 0, j)),
            pl.BlockSpec((sides, 1, rows, tile), lambda k, j: (0, k + 1, 0, j)),
            pl.BlockSpec((sides, 2, rows, out), lambda k, j: (0, 0, 0, 0)),
        ],
        out_specs=pl.BlockSpec((tile, out), lambda k, j: (k * per + j, 0)),
        compiler_params=params(),
        name="conv_weight_grad",
    )(pieces, pieces, low)


def local(
    section_input,
    norm1_gain,
    norm1_bias,
    conv1_weight,
    conv1_bias,
    norm2_gain,
    norm2_bias,
    conv2_weight,
    conv2_bias,
    pool_weight,
    out_grad,
    clip_table,
    clip_index,
):
    micro_count, seq_count, local_rows, local_in = section_input.shape
    batch_count, pos_count, ch_count = (lax.axis_size(a) for a in ("batch", "pos", "ch"))
    batch, pos, ch = (lax.axis_index(a) for a in ("batch", "pos", "ch"))
    total_rows = seq_count * local_rows * batch_count * pos_count
    wide_in = 2 * local_in
    local_out = conv1_weight.shape[1]
    wide_out = 2 * local_out
    half = local_rows // 2
    pairs = half // 2
    plane = batch_count * pos_count
    spot = batch * pos_count + pos
    swap = [(0, 1), (1, 0)]
    is_low = ch == 0

    def other_ch(v):
        return lax.ppermute(v, "ch", swap)

    def natural(own, other, axis):
        return jnp.where(
            is_low,
            jnp.concatenate([own, other], axis=axis),
            jnp.concatenate([other, own], axis=axis),
        )

    x = section_input.reshape(micro_count, local_rows, local_in)

    def fetch(w):
        rows = w.shape[0] // plane
        piece = lax.dynamic_slice_in_dim(w, spot * rows, rows, axis=0)
        return lax.all_gather(other_ch(piece), ("batch", "pos"), axis=0, tiled=True)

    w1_other = fetch(conv1_weight)
    w2_other = fetch(conv2_weight)
    wp_other = fetch(pool_weight)

    up = [(i, i + 1) for i in range(pos_count - 1)]
    down = [(j, i) for i, j in up]
    before = lax.ppermute(x[:, -RIM:], "pos", up)
    after = lax.ppermute(x[:, :RIM], "pos", down)
    pad = jnp.zeros((micro_count, 16 - 2 * RIM, local_in), BF16)
    x_ext = jnp.concatenate([before, x, after, pad], axis=1)
    x_full = natural(x_ext, other_ch(x_ext), 2)

    x32 = x.astype(F32)
    lead = spot == 0
    stats = jnp.concatenate(
        [
            jnp.sum(x32, axis=1),
            jnp.sum(x32 * x32, axis=1),
            jnp.where(lead, jnp.stack([norm1_gain, norm1_bias]), 0.0),
        ]
    )
    small = jnp.stack([conv1_bias, norm2_gain, norm2_bias, conv2_bias])
    small = jnp.where(lead, small, 0.0)
    stats = natural(stats, jnp.zeros_like(stats), 1)
    small = natural(small, jnp.zeros_like(small), 1)
    stats = jnp.concatenate([stats, jnp.zeros((stats.shape[0], wide_out - wide_in), F32)], axis=1)
    summed = reduce_all(jnp.concatenate([stats, small]), 1)
    moments = summed[: 2 * micro_count, :wide_in] / total_rows
    gain1, bias1 = summed[2 * micro_count, :wide_in], summed[2 * micro_count + 1, :wide_in]
    small = summed[2 * micro_count + 2 :]
    center1 = moments[:micro_count]
    inverse1 = lax.rsqrt(moments[micro_count:] - center1 * center1 + EPS)

    def own_first(v):
        return jnp.where(
            is_low, v, jnp.concatenate([v[..., local_out:], v[..., :local_out]], axis=-1)
        )

    small = own_first(small)
    vec1 = jnp.stack(
        [center1, inverse1 * gain1, jnp.broadcast_to(bias1, center1.shape), inverse1]
        + [jnp.zeros_like(center1)] * 4,
        axis=1,
    )
    who = jnp.stack([ch, pos * local_rows, pos_count * local_rows]).astype(jnp.int32)
    pieces, x_split = make_hidden(who, x_full, vec1, half)

    first_own, stat_own = conv_forward(pieces[0], conv1_weight, small[0, :local_out])
    first_other, stat_other = conv_forward(pieces[0], w1_other, small[0, local_out:])
    stats2 = jnp.concatenate([stat_own[: 2 * micro_count], stat_other[: 2 * micro_count]], axis=1)

    def to_natural(v):
        return own_first(v)

    summed2 = own_first(reduce_all(to_natural(stats2), 2)) / total_rows
    center2 = summed2[0::2]
    inverse2 = lax.rsqrt(summed2[1::2] - center2 * center2 + EPS)
    spread = lambda v: jnp.broadcast_to(v, center2.shape)
    vec2 = jnp.stack(
        [center2, inverse2, spread(small[1]), spread(small[2]), spread(small[3])]
        + [jnp.zeros_like(center2)] * 3,
        axis=1,
    )

    def own_rows(w):
        return jnp.where(is_low, w, jnp.concatenate([w[local_out:], w[:local_out]], axis=0))

    w2 = jnp.concatenate([own_rows(conv2_weight), own_rows(w2_other)], axis=1)
    wp = jnp.concatenate([own_rows(pool_weight), own_rows(wp_other)], axis=1)

    bins = local_rows // 2
    mine = bins // 2
    og = out_grad.reshape(micro_count, bins, local_out)
    og_own = lax.dynamic_slice_in_dim(og, ch * mine, mine, axis=1)
    og_away = lax.dynamic_slice_in_dim(og, (1 - ch) * mine, mine, axis=1)
    og_full = jnp.concatenate([og_own, other_ch(og_away)], axis=2)
    table_pos = jnp.arange(clip_table.shape[0], dtype=jnp.int32)
    limit = jnp.sum(jnp.where(table_pos[None] == clip_index[:, None], clip_table[None], 0.0), axis=1)
    limits = jnp.broadcast_to(limit[:, None, None], (micro_count, 8, 128))

    pooled, hid2, branch, diff, lg, a2g, sg, sums3 = middle(
        first_own, first_other, vec2, w2, wp, og_full.reshape(micro_count, 1, mine, wide_out), limits
    )

    pooled_away = other_ch(pooled[:, :, local_out:])
    section_output = natural(pooled[:, :, :local_out], pooled_away, 1)
    section_output = section_output.reshape(micro_count, seq_count, bins, local_out)

    sums3 = sums3[:, :3].reshape(3 * micro_count, wide_out)
    sums3 = own_first(reduce_all(to_natural(sums3), 3)).reshape(micro_count, 3, wide_out)
    gain2 = small[1]
    mean_grad = (sums3[:, 0] / total_rows)[None, :, None]
    mean_cross = (sums3[:, 1] / total_rows)[None, :, None]
    normed = jnp.concatenate([first_own, first_other], axis=-1) - center2[None, :, None]
    normed = normed * inverse2[None, :, None]
    first_low = sg + (inverse2 * gain2)[None, :, None] * (a2g - mean_grad - normed * mean_cross)
    first_low = first_low.astype(BF16)
    low_sum = jnp.sum(first_low.astype(F32), axis=2)
    low_sum = low_sum[0] + low_sum[1]

    def turned(v):
        return jnp.where(is_low, v, jnp.concatenate([v[..., local_out:], v[..., :local_out]], axis=-1))

    line = pos_count * ch_count
    up = [(i, i + 1) for i in range(line - 1)]
    down = [(j, i) for i, j in up]
    last = lax.ppermute(turned(first_low[:, :, -1:]), ("pos", "ch"), up)
    head = lax.ppermute(turned(first_low[:, :, :1]), ("pos", "ch"), down)
    longer = jnp.concatenate([turned(last), first_low, turned(head)], axis=2)
    grad_pieces = jnp.stack(
        [longer[d % 2, :, d // 2 : d // 2 + pairs] for d in range(PIECES)]
    )
    a1g, sums4 = conv_back(grad_pieces, conv1_weight, w1_other, x_split[0], vec1)

    low_away = other_ch(first_low[..., local_out:])
    low_both = jnp.stack([first_low[..., :local_out], low_away])
    dw1 = conv_weight_grad(pieces, low_both)

    def split_grad(left, right):
        left = own_first(left)
        grad = jnp.einsum("mrc,mro->co", left, right, preferred_element_type=F32)
        away = other_ch(grad[:, local_out:].astype(BF16))
        return (grad[:, :local_out] + away.astype(F32)).astype(BF16)

    dw2 = split_grad(hid2, branch)
    dwp = split_grad(diff, lg)

    def scatter(v):
        return lax.psum_scatter(v, ("batch", "pos"), scatter_dimension=0, tiled=True).astype(F32)

    part = jnp.concatenate(
        [sums4[: 2 * micro_count], jnp.zeros((2 * micro_count, wide_out - wide_in), F32)], axis=1
    )
    part = jnp.concatenate([part, to_natural(low_sum)])
    part = reduce_all(part, 4)
    one = part[: 2 * micro_count, :wide_in]
    grad_sum, cross_sum = one[0::2], one[1::2]
    normed1 = (x_split[0].astype(F32) - center1[None, :, None]) * inverse1[None, :, None]
    dx = (inverse1 * gain1)[None, :, None] * (
        a1g - (grad_sum / total_rows)[None, :, None] - normed1 * (cross_sum / total_rows)[None, :, None]
    )
    dx = jnp.stack([dx[0], dx[1]], axis=2).reshape(micro_count, half, wide_in).astype(BF16)
    dx_own = lax.dynamic_slice_in_dim(dx, ch * local_in, local_in, axis=2)
    dx_away = other_ch(lax.dynamic_slice_in_dim(dx, (1 - ch) * local_in, local_in, axis=2))
    input_grad = natural(dx_own, dx_away, 1).reshape(section_input.shape)

    def mine_of(v, width):
        return lax.dynamic_slice_in_dim(v, ch * width, width, axis=0)

    return (
        section_output,
        input_grad,
        mine_of(jnp.sum(cross_sum, axis=0), local_in),
        mine_of(jnp.sum(grad_sum, axis=0), local_in),
        scatter(dw1),
        mine_of(jnp.sum(part[2 * micro_count :], axis=0), local_out),
        jnp.sum(sums3[:, 1], axis=0)[:local_out],
        jnp.sum(sums3[:, 0], axis=0)[:local_out],
        scatter(dw2),
        jnp.sum(sums3[:, 2], axis=0)[:local_out],
        scatter(dwp),
    )


def solution(mesh):
    placed = (
        P(None, "batch", "pos", "ch"),
        P("ch"),
        P("ch"),
        P(None, "ch"),
        P("ch"),
        P("ch"),
        P("ch"),
        P(None, "ch"),
        P("ch"),
        P(None, "ch"),
        P(None, "batch", "pos", "ch"),
        P(),
        P(),
    )
    return jax.shard_map(
        local,
        mesh=mesh,
        in_specs=placed,
        out_specs=(
            P(None, "batch", "pos", "ch"),
            P(None, "batch", "pos", "ch"),
            P("ch"),
            P("ch"),
            P(("batch", "pos"), "ch"),
            P("ch"),
            P("ch"),
            P("ch"),
            P(("batch", "pos"), "ch"),
            P("ch"),
            P(("batch", "pos"), "ch"),
        ),
        check_vma=False,
    )
```

time: 2410 us -> 701 us (0.29)
  local copies, waits for them, and re-layouts: 869 us -> 80.2 us
  other arithmetic: 511 us -> 66.8 us
  Pallas kernels: 0 us -> 303 us
  blocking collectives: 269 us -> 0 us
  waiting for transfers between devices: 455 us -> 191 us
  matrix products: 187 us -> 10.7 us
  starting transfers between devices: 87.1 us -> 24.9 us
    unnamed x211 -> x65, local copies, waits for them, and re-layouts: 396 us -> 12.8 us
    unnamed x14 -> x1, other arithmetic: 351 us -> 3.08 us
    pallas_call x0 -> x10, Pallas kernels: none -> 303 us  [the longest x4 147 us: reduce_all(): pl.pallas_call(reduce_kernel, out_shape=jax.ShapeDtypeStruct(shape, F32),...]
    psum x7 -> x0, blocking collectives: 269 us -> none  [the longest x2 69 us: local(): sums_one = lax.psum(moments(inputs), ('batch', 'pos'))]
    all_gather x6 -> x3, waiting for transfers between devices: 207 us -> 0.01 us  [fetch(): return lax.all_gather(other_ch(piece), ('batch', 'pos'), axis=0, tiled=True)]
    ppermute x8 -> x14, waiting for transfers between devices: 1.42 us -> 191 us  [the longest x10 186 us: other_ch(): return lax.ppermute(v, 'ch', swap)]
    dot_general x34 -> x2, matrix products: 187 us -> 10.7 us  [split_grad(): grad = jnp.einsum('mrc,mro->co', left, right, preferred_element_type=F32)]
    another operation x16 -> x22, local copies, waits for them, and re-layouts: 148 us -> 7.79 us  [the longest x6 4.06 us: local(): jnp.stack([center1, inverse1 * gain1, jnp.broadcast_to(bias1, center1.sha...]
  transfers between devices with their start and end apart: 35 -> 20, of which waited for: 15 -> 9; matrix products, arithmetic and copies ran while one was open for 51% -> 19% of each run, Pallas kernels for 0% -> 32%
where the time goes in v1:
time: 701 us; the launch traced here: 691 us
  Pallas kernels  303 us (43%)
  waiting for transfers between devices  191 us (27%)
  local copies, waits for them, and re-layouts  80.2 us (11%)
  other arithmetic  66.8 us (10%)
  starting transfers between devices  24.9 us (4%)
  between operations  15.1 us (2%)
  matrix products  10.7 us (2%)
    ppermute x10, waiting for transfers between devices, other_ch(): return lax.ppermute(v, 'ch', swap)  186 us
    pallas_call x4, Pallas kernels, reduce_all(): pl.pallas_call(reduce_kernel, out_shape=jax.ShapeDtypeStruct(shape, F32),...  147 us
    pallas_call x1, Pallas kernels, middle(): pl.pallas_call(middle_kernel, out_shape=(jax.ShapeDtypeStruct((micro_coun...  41.4 us
    pallas_call x1, Pallas kernels, conv_weight_grad(): pl.pallas_call(weight_kernel, out_shape=jax.ShapeDtypeStruct((KW * wide,...  33.3 us
    pallas_call x2, Pallas kernels, conv_forward(): pl.pallas_call(conv_kernel, out_shape=(jax.ShapeDtypeStruct((2, micro_cou...  32.2 us
    pallas_call x1, Pallas kernels, conv_back(): pl.pallas_call(back_kernel, out_shape=(jax.ShapeDtypeStruct((2, micro_cou...  32.1 us
    ppermute x10, starting transfers between devices, other_ch(): return lax.ppermute(v, 'ch', swap)  17.3 us
    pallas_call x1, Pallas kernels, make_hidden(): pl.pallas_call(hidden_kernel, out_shape=(jax.ShapeDtypeStruct((2, PIECES,...  16.7 us
  transfers between devices with their start and end apart: 20, of which 9 were waited for; matrix products, arithmetic and copies ran while one was open for 19% of the time, Pallas kernels for 32%

profile of v1, /device:TPU:0, one launch (start us, length us, event | category | flops | bytes accessed | tf_op | source)
XLA Modules:
  0.0 691.1 jit_solution(3730504342354083936)
XLA Ops:
  8.3 3.0 collective-permute-start.4
  11.4 3.8 collective-permute-done.4
  18.7 3.4 collective-permute-done.5
  25.8 12.2 %collective-permute-done.3 = bf16[400,768]{1,0:T(8,128)(2,1)S(1)} collective-permute-done((bf16[400,768]{1,0:T(8,128)(2,1)S(1)}, bf16[400,768]{1,0:T(8,128)(2,1)S(1)}, u32[]{:S(2)}, u32[]{:S(2)}) %collective-permute-start.3) | collective-permute-done | bytes 614432 | tf_op jit(solution)/shard_map/ppermute | solution.py:478
  46.9 41.8 %shard_map.212 = f32[16,1536]{1,0:T(8,128)} custom-call(f32[16,1536]{1,0:T(8,128)} %pad.21.v_ref), custom_call_target="tpu_custom_call" | custom-call | tf_op jit(solution)/shard_map/pallas_call | solution.py:88
  92.5 13.7 %concatenate.157 = bf16[2,1040,640]{2,1,0:T(8,128)(2,1)S(1)} concatenate(bf16[2,2,640]{2,1,0:T(2,128)(2,1)S(1)} %collective-permute-done, bf16[2,1024,640]{2,1,0:T(8,128)(2,1)} %bitcast.62, bf16[2,2,640]{2,1,0:T(2,128)(2,1)} %collective-permute-done.1, bf16[2,12,640]{2,1,0:T(8,128)(2,1)S(1)} %broadcast_in_dim.24), dimensions={1} | concatenate | bytes 5324800 | tf_op jit(solution)/shard_map/concatenate | solution.py:503
  124.2 41.5 %collective-permute-done.2 = bf16[2,1040,640]{2,1,0:T(8,128)(2,1)} collective-permute-done((bf16[2,1040,640]{2,1,0:T(8,128)(2,1)S(1)}, bf16[2,1040,640]{2,1,0:T(8,128)(2,1)}, u32[]{:S(2)}, u32[]{:S(2)}) %collective-permute-start.2) | collective-permute-done | bytes 2662432 | tf_op jit(solution)/shard_map/ppermute | solution.py:478
  165.7 6.4 maximum_select_fusion.x_ref
  172.1 16.7 %hidden.1 = (bf16[2,6,2,256,1280]{4,3,2,1,0:T(8,128)(2,1)}, bf16[2,2,2,256,1280]{4,3,2,1,0:T(8,128)(2,1)}) custom-call(s32[3]{0:T(128)} %pad_add_fusion.who, bf16[2,1040,1280]{2,1,0:T(8,128)(2,1)} %maximum_select_fusion.x_ref, f32[2,8,1280]{2,1,0:T(8,128)} %stack.93.vec_ref), custom_call_target="tpu_custom_call" | custom-call | tf_op jit(solution)/shard_map/hidden/pallas_call | solution.py:150
  188.8 7.0 %slice.282 = bf16[1,6,2,256,1280]{4,3,2,1,0:T(8,128)(2,1)} slice(bf16[2,6,2,256,1280]{4,3,2,1,0:T(8,128)(2,1)} %get-tuple-element.27), slice={[0:1], [0:6], [0:2], [0:256], [0:1280]} | slice | bytes 15728640 | tf_op jit(solution)/shard_map/slice | solution.py:541
  195.8 16.1 %conv_forward.2 = (f32[2,2,256,768]{3,2,1,0:T(8,128)}, f32[8,768]{1,0:T(8,128)}) custom-call(bf16[6,512,1280]{2,1,0:T(8,128)(2,1)} %bitcast.57, bf16[6400,768]{1,0:T(8,128)(2,1)} %w_ref.1, f32[1,768]{1,0:T(1,128)} %get-tuple-element.137.b_ref), custom_call_target="tpu_custom_call" | custom-call | tf_op jit(solution)/shard_map/conv_forward/pallas_call | solution.py:200
  227.0 16.1 %conv_forward.3 = (f32[2,2,256,768]{3,2,1,0:T(8,128)}, f32[8,768]{1,0:T(8,128)}) custom-call(bf16[6,512,1280]{2,1,0:T(8,128)(2,1)} %bitcast.58, bf16[6400,768]{1,0:T(8,128)(2,1)} %all-gather.4.cloned.1.call-done.w_ref, f32[1,768]{1,0:T(1,128)} %get-tuple-element.136.b_ref), custom_call_target="tpu_custom_call" | custom-call | tf_op jit(solution)/shard_map/conv_forward/pallas_call | solution.py:200
  244.5 21.1 %shard_map.213 = f32[8,1536]{1,0:T(8,128)} custom-call(f32[8,1536]{1,0:T(8,128)} %pad.22.v_ref), custom_call_target="tpu_custom_call" | custom-call | tf_op jit(solution)/shard_map/pallas_call | solution.py:88
  268.8 41.4 %middle.1 = (bf16[2,256,1536]{2,1,0:T(8,128)(2,1)}, bf16[2,512,1536]{2,1,0:T(8,128)(2,1)}, bf16[2,512,1536]{2,1,0:T(8,128)(2,1)}, bf16[2,256,1536]{2,1,0:T(8,128...) custom-call(f32[2,2,256,768]{3,2,1,0:T(8,128)} %get-tuple-element.28, ...), custom_call_target="tpu_custom_call" | custom-call | tf_op jit(solution)/shard_map/middle/pallas_call | solution.py:323
  319.2 50.4 %collective-permute-done.13 = bf16[1536,768]{1,0:T(8,128)(2,1)S(1)} collective-permute-done((bf16[1536,768]{1,0:T(8,128)(2,1)S(1)}, bf16[1536,768]{1,0:T(8,128)(2,1)S(1)}, u32[]{:S(2)}, u32[]{:S(2)}) %collective-permute-start.13) | collective-permute-done | bytes 2359328 | tf_op jit(solution)/shard_map/ppermute | solution.py:478
  371.9 8.0 %convolution_bitcast_fusion.1 = f32[1536,1536]{1,0:T(8,128)S(1)} fusion(bf16[2,512,1536]{2,1,0:T(8,128)(2,1)} %get-tuple-element.40, bf16[2,512,1536]{2,1,0:T(8,128)(2,1)S(1)} %copy-done.10, bf16[2,512,768]{2,1,0:T(8,128)(2,1)} %get-tuple-element.93, bf16[2,512,768]{2,1,0:T(8,128)(2,1)} %get-tuple-element.92, pred[]{:T(512)S(6)} %eq.19), kind=kOutput, calls=%fused_computation.5 | convolution fusion | flops 4839702528 | bytes 18874368 | tf_op jit(solution)/shard_map/mrc,mro->co/dot_general | solution.py:614
  380.0 3.5 copy-done.8
  386.3 61.1 %shard_map.214 = f32[8,1536]{1,0:T(8,128)} custom-call(f32[8,1536]{1,0:T(8,128)} %pad.23.v_ref), custom_call_target="tpu_custom_call" | custom-call | tf_op jit(solution)/shard_map/pallas_call | solution.py:88
  448.2 5.0 fusion.10
  453.4 7.6 %convert_reduce_fusion.1 = (f32[2,2,1536]{2,1,0:T(2,128)S(1)}, bf16[2,2,256,1536]{3,2,1,0:T(8,128)(2,1)S(1)}) fusion(f32[2,2,256,1536]{3,2,1,0:T(8,128)} %get-tuple-element.33, f32[2,1536]{1,0:T(2,128)S(1)} %bitcast.69, f32[2,1536]{1,0:T(2,128)S(1)} %get-tuple-element.89, f32[2,1536]{1,0:T(2,128)S(1)} %slice.293, ...), kind=kLoop, calls=%fused_computation.15 | loop fusion | flops 17295360 | bytes 22106112 | tf_op jit(solution)/shard_map/reduce_sum | solution.py:591
  463.6 35.2 %collective-permute-done.11 = bf16[2,2,256,768]{3,2,1,0:T(8,128)(2,1)S(1)} collective-permute-done((bf16[2,2,256,768]{3,2,1,0:T(8,128)(2,1)S(1)}, bf16[2,2,256,768]{3,2,1,0:T(8,128)(2,1)S(1)}, u32[]{:S(2)}, u32[]{:S(2)}) %collective-permute-start.11) | collective-permute-done | bytes 1572896 | tf_op jit(solution)/shard_map/ppermute | solution.py:478
  500.8 33.3 %conv_weight_grad.1 = bf16[6400,768]{1,0:T(8,128)(2,1)} custom-call(bf16[2,6,512,1280]{3,2,1,0:T(8,128)(2,1)} %bitcast.55, bf16[2,6,512,1280]{3,2,1,0:T(8,128)(2,1)} %bitcast.56, bf16[2,2,512,768]{3,2,1,0:T(8,128)(2,1)} %pad_maximum_fusion.4.f_ref), custom_call_target="tpu_custom_call" | custom-call | tf_op jit(solution)/shard_map/conv_weight_grad/pallas_call | solution.py:433
  534.1 3.4 slice_bitcast_fusion.x_ref
  537.7 3.5 collective-permute-start.8
  542.7 4.2 collective-permute-done.9
  547.1 5.2 fusion
  552.3 32.1 %conv_back.1 = (f32[2,2,256,1280]{3,2,1,0:T(8,128)}, f32[8,1280]{1,0:T(8,128)}) custom-call(bf16[6,512,1536]{2,1,0:T(8,128)(2,1)} %bitcast.61, bf16[5,1280,768]{2,1,0:T(8,128)(2,1)} %bitcast.59, bf16[5,1280,768]{2,1,0:T(8,128)(2,1)} %bitcast.60, bf16[2,2,256,1280]{3,2,1,0:T(8,128)(2,1)} %slice_bitcast_fusion.x_ref, f32[2,8,1280]{2,1,0:T(8,128)} %stack.93.vec_ref), custom_call_target="tpu_custom_call" | custom-call | tf_op jit(solution)/shard_map/conv_back/pallas_call | solution.py:389
  585.9 23.0 %shard_map.215 = f32[8,1536]{1,0:T(8,128)} custom-call(f32[8,1536]{1,0:T(8,128)} %pad.24.v_ref), custom_call_target="tpu_custom_call" | custom-call | tf_op jit(solution)/shard_map/pallas_call | solution.py:88
  609.8 4.6 multiply_convert_fusion
  627.1 39.7 %collective-permute-done.7 = bf16[2,256,768]{2,1,0:T(8,128)(2,1)} collective-permute-done((bf16[2,256,768]{2,1,0:T(8,128)(2,1)}, bf16[2,256,768]{2,1,0:T(8,128)(2,1)}, u32[]{:S(2)}, u32[]{:S(2)}) %collective-permute-start.7) | collective-permute-done | bytes 786464 | tf_op jit(solution)/shard_map/ppermute | solution.py:478
  666.8 3.1 fusion.14
  669.9 6.9 broadcast_select_fusion
  (212 shorter events, 101.7 us)
Async XLA Ops:
  7.2 31.7 %copy-start = (bf16[2,1,1024,640]{3,2,1,0:T(8,128)(2,1)S(1)}, bf16[2,1,1024,640]{3,2,1,0:T(8,128)(2,1)}, u32[]{:S(2)}) copy-start(bf16[2,1,1024,640]{3,2,1,0:T(8,128)(2,1)} %param.13) | copy-start | bytes 7864324
  7.2 206.0 %all-gather.6.cloned.1.call-start = ((), (), s32[]{:S(2)}) async-start(), calls=%async_computation.4 | async-start | bytes 2506752 | tf_op jit(solution)/shard_map/all_gather | solution.py:492
  8.3 6.9 collective-permute-start.4
  15.9 200.1 %all-gather.8.cloned.1.call-start = ((), (), s32[]{:S(2)}) async-start(), calls=%async_computation.5 | async-start | bytes 2506752 | tf_op jit(solution)/shard_map/all_gather | solution.py:492
  16.9 28.5 %copy-start.29 = (f32[640]{0:T(1024)S(1)}, f32[640]{0:T(1024)}, u32[]{:S(2)}) copy-start(f32[640]{0:T(1024)} %param.14) | copy-start | bytes 7684
  16.9 28.5 %copy-start.30 = (f32[640]{0:T(1024)S(1)}, f32[640]{0:T(1024)}, u32[]{:S(2)}) copy-start(f32[640]{0:T(1024)} %param.15) | copy-start | bytes 7684
  16.9 28.5 %copy-start.25 = (f32[768]{0:T(1024)S(1)}, f32[768]{0:T(1024)}, u32[]{:S(2)}) copy-start(f32[768]{0:T(1024)} %param.17) | copy-start | bytes 9220
  16.9 28.5 %copy-start.26 = (f32[768]{0:T(1024)S(1)}, f32[768]{0:T(1024)}, u32[]{:S(2)}) copy-start(f32[768]{0:T(1024)} %param.18) | copy-start | bytes 9220
  16.9 28.5 %copy-start.27 = (f32[768]{0:T(1024)S(1)}, f32[768]{0:T(1024)}, u32[]{:S(2)}) copy-start(f32[768]{0:T(1024)} %param.19) | copy-start | bytes 9220
  16.9 28.5 %copy-start.28 = (f32[768]{0:T(1024)S(1)}, f32[768]{0:T(1024)}, u32[]{:S(2)}) copy-start(f32[768]{0:T(1024)} %param.21) | copy-start | bytes 9220
  16.9 5.2 collective-permute-start.5
  22.8 204.1 %all-gather.4.cloned.1.call-start = ((), (), s32[]{:S(2)}) async-start(), calls=%async_computation.3 | async-start | bytes 10444800 | tf_op jit(solution)/shard_map/all_gather | solution.py:492
  24.0 14.0 %collective-permute-start.3 = (bf16[400,768]{1,0:T(8,128)(2,1)S(1)}, bf16[400,768]{1,0:T(8,128)(2,1)S(1)}, u32[]{:S(2)}, u32[]{:S(2)}) collective-permute-start(bf16[400,768]{1,0:T(8,128)(2,1)S(1)} %constant_dynamic-slice_fusion.3), channel_id=1, source_target_pairs={{0,1},{1,0},{2,3},{3,2},{4,5},{5,4},{6,7},{7,6},{8,9},{9,8},{10,11... | collective-permute-start | bytes 1843208 | tf_op jit(solution)/shard_map/ppermute | solution.py:478
  38.9 639.8 %reduce-scatter.8.cloned.1.call-start = ((), (), s32[]{:S(2)}) async-start(), calls=%async_computation.8 | async-start | bytes 2506752 | tf_op jit(solution)/shard_map/reduce_scatter | solution.py:622
  38.9 53.5 %collective-permute-start = (bf16[2,2,640]{2,1,0:T(2,128)(2,1)S(1)}, bf16[2,2,640]{2,1,0:T(2,128)(2,1)S(1)}, u32[]{:S(2)}, u32[]{:S(2)}) collective-permute-start(bf16[2,2,640]{2,1,0:T(2,128)(2,1)S(1)} %get-tuple-element.107), channel_id=1, source_target_pairs={{0,2},{2,4},{4,6},{6,8},{8,10},{10,12},{12,14},{1,3},{3,5},{5,7},{... | collective-permute-start | bytes 15368 | tf_op jit(solution)/shard_map/ppermute | solution.py:500
  40.2 52.2 %collective-permute-start.1 = (bf16[2,2,640]{2,1,0:T(2,128)(2,1)S(1)}, bf16[2,2,640]{2,1,0:T(2,128)(2,1)}, u32[]{:S(2)}, u32[]{:S(2)}) collective-permute-start(bf16[2,2,640]{2,1,0:T(2,128)(2,1)S(1)} %get-tuple-element.106), channel_id=1, source_target_pairs={{2,0},{4,2},{6,4},{8,6},{10,8},{12,10},{14,12},{3,1},{5,3},{7,5},{... | collective-permute-start | bytes 15368 | tf_op jit(solution)/shard_map/ppermute | solution.py:501
  44.2 77.7 %collective-permute-start.6 = (bf16[2,256,768]{2,1,0:T(8,128)(2,1)}, bf16[2,256,768]{2,1,0:T(8,128)(2,1)}, u32[]{:S(2)}, u32[]{:S(2)}) collective-permute-start(bf16[2,256,768]{2,1,0:T(8,128)(2,1)} %get-tuple-element.121), channel_id=1, source_target_pairs={{0,1},{1,0},{2,3},{3,2},{4,5},{5,4},{6,7},{7,6},{8,9},{9,8},{10,11... | collective-permute-start | bytes 2359304 | tf_op jit(solution)/shard_map/ppermute | solution.py:478
  106.2 59.5 %collective-permute-start.2 = (bf16[2,1040,640]{2,1,0:T(8,128)(2,1)S(1)}, bf16[2,1040,640]{2,1,0:T(8,128)(2,1)}, u32[]{:S(2)}, u32[]{:S(2)}) collective-permute-start(bf16[2,1040,640]{2,1,0:T(8,128)(2,1)S(1)} %concatenate.157), channel_id=1, source_target_pairs={{0,1},{1,0},{2,3},{3,2},{4,5},{5,4},{6,7},{7,6},{8,9},{9,8},{10,11... | collective-permute-start | bytes 7987208 | tf_op jit(solution)/shard_map/ppermute | solution.py:478
  227.0 40.3 %copy-start.19 = (f32[1536]{0:T(1024)S(1)}, f32[1536]{0:T(1024)}, u32[]{:S(2)}) copy-start(f32[1536]{0:T(1024)} %get-tuple-element.85) | copy-start | bytes 18436
  227.0 40.4 %copy-start.23 = (f32[1536]{0:T(1024)S(1)}, f32[1536]{0:T(1024)}, u32[]{:S(2)}) copy-start(f32[1536]{0:T(1024)} %get-tuple-element.84) | copy-start | bytes 18436
  227.0 40.4 %copy-start.22 = (f32[1536]{0:T(1024)S(1)}, f32[1536]{0:T(1024)}, u32[]{:S(2)}) copy-start(f32[1536]{0:T(1024)} %get-tuple-element.83) | copy-start | bytes 18436
  315.6 54.0 %collective-permute-start.13 = (bf16[1536,768]{1,0:T(8,128)(2,1)S(1)}, bf16[1536,768]{1,0:T(8,128)(2,1)S(1)}, u32[]{:S(2)}, u32[]{:S(2)}) collective-permute-start(bf16[1536,768]{1,0:T(8,128)(2,1)S(1)} %slice.439), channel_id=1, source_target_pairs={{0,1},{1,0},{2,3},{3,2},{4,5},{5,4},{6,7},{7,6},{8,9},{9,8},{10,11... | collective-permute-start | bytes 7077896 | tf_op jit(solution)/shard_map/ppermute | solution.py:478
  371.9 308.4 %reduce-scatter.6.cloned.1.call-start = ((), (), s32[]{:S(2)}) async-start(), calls=%async_computation.7 | async-start | bytes 2506752 | tf_op jit(solution)/shard_map/reduce_scatter | solution.py:622
  383.8 64.4 %collective-permute-start.12 = (bf16[1536,768]{1,0:T(8,128)(2,1)S(1)}, bf16[1536,768]{1,0:T(8,128)(2,1)}, u32[]{:S(2)}, u32[]{:S(2)}) collective-permute-start(bf16[1536,768]{1,0:T(8,128)(2,1)S(1)} %slice.440), channel_id=1, source_target_pairs={{0,1},{1,0},{2,3},{3,2},{4,5},{5,4},{6,7},{7,6},{8,9},{9,8},{10,11... | collective-permute-start | bytes 7077896 | tf_op jit(solution)/shard_map/ppermute | solution.py:478
  453.2 228.7 %reduce-scatter.4.cloned.1.call-start = ((), (), s32[]{:S(2)}) async-start(), calls=%async_computation.6 | async-start | bytes 10444800 | tf_op jit(solution)/shard_map/reduce_scatter | solution.py:622
  461.3 37.6 %collective-permute-start.11 = (bf16[2,2,256,768]{3,2,1,0:T(8,128)(2,1)S(1)}, bf16[2,2,256,768]{3,2,1,0:T(8,128)(2,1)S(1)}, u32[]{:S(2)}, u32[]{:S(2)}) collective-permute-start(bf16[2,2,256,768]{3,2,1,0:T(8,128)(2,1)S(1)} %get-tuple-element.95), channel_id=1, source_target_pairs={{0,1},{1,0},{2,3},{3,2},{4,5},{5,4},{6,7},{7,6},{8,9},{9,8},{10,11... | collective-permute-start | bytes 4718600 | tf_op jit(solution)/shard_map/ppermute | solution.py:478
  537.7 5.0 collective-permute-start.8
  541.2 5.7 collective-permute-start.9
  552.3 57.5 %copy-start.18 = (f32[2,1280]{1,0:T(2,128)S(1)}, f32[2,1280]{1,0:T(2,128)}, u32[]{:S(2)}) copy-start(f32[2,1280]{1,0:T(2,128)} %copy-done.17) | copy-start | bytes 30724
  552.3 57.5 %copy-start.21 = (f32[2,1280]{1,0:T(2,128)S(1)}, f32[2,1280]{1,0:T(2,128)}, u32[]{:S(2)}) copy-start(f32[2,1280]{1,0:T(2,128)} %get-tuple-element.138) | copy-start | bytes 30724
  619.4 50.5 %collective-permute-start.10 = (bf16[2,512,640]{2,0,1:T(2,128)(2,1)S(1)}, bf16[2,512,640]{2,0,1:T(2,128)(2,1)}, u32[]{:S(2)}, u32[]{:S(2)}) collective-permute-start(bf16[2,512,640]{2,0,1:T(2,128)(2,1)S(1)} %get-tuple-element.103), channel_id=1, source_target_pairs={{0,1},{1,0},{2,3},{3,2},{4,5},{5,4},{6,7},{7,6},{8,9},{9,8},{10,11... | collective-permute-start | bytes 3932168 | tf_op jit(solution)/shard_map/ppermute | solution.py:478
  621.7 45.1 %collective-permute-start.7 = (bf16[2,256,768]{2,1,0:T(8,128)(2,1)}, bf16[2,256,768]{2,1,0:T(8,128)(2,1)}, u32[]{:S(2)}, u32[]{:S(2)}) collective-permute-start(bf16[2,256,768]{2,1,0:T(8,128)(2,1)} %get-tuple-element.119), channel_id=1, source_target_pairs={{0,1},{1,0},{2,3},{3,2},{4,5},{5,4},{6,7},{7,6},{8,9},{9,8},{10,11... | collective-permute-start | bytes 2359304 | tf_op jit(solution)/shard_map/ppermute | solution.py:478
  (19 other events, 73.5 us)
Sparse Core Ops, SparseCore 0:
  16.0 43.6 all-gather.5
  62.6 48.9 all-gather.7
  113.9 82.6 all-gather.3
  372.0 63.7 reduce-scatter.7
  453.3 64.6 reduce-scatter.5
  534.2 126.4 reduce-scatter.3

commit v2 on v1

--- a/solution.py
+++ b/solution.py
@@ -36,71 +36,113 @@
     return 0.5 * (1.0 + t) + 0.5 * u * (1.0 - t * t) * (C0 + (3.0 * C0 * C1) * square)
 
 
-def reduce_kernel(v_ref, o_ref, near, mid, far, near_send, near_recv, far_send, far_recv):
-    batch, pos, ch = (lax.axis_index(a) for a in ("batch", "pos", "ch"))
-    pos_count = lax.axis_size("pos")
-    me = batch * 2 + ch
+class Reduce:
+    def __init__(self, value, core_in, near, far, result, sems):
+        self.value, self.core_in, self.near, self.far, self.result = value, core_in, near, far, result
+        self.send, self.recv = sems
+        self.batch, self.pos, self.ch = (lax.axis_index(a) for a in ("batch", "pos", "ch"))
+        self.core = lax.rem(self.pos, 2)
+        self.z = self.pos // 2
+        self.far_count = lax.axis_size("pos") // 2
+        half = value.shape[1] // 2
+        self.mine = pl.ds(pl.multiple_of(self.core * half, half), half)
+        self.away = pl.ds(pl.multiple_of((1 - self.core) * half, half), half)
+        self.me = self.batch * 2 + self.ch
+        self.core_peer = (self.batch, self.z * 2 + 1 - self.core, self.ch)
+        self.near_peers = []
+        for step in range(1, 4):
+            other = lax.rem(self.me + step, 4)
+            self.near_peers.append((other // 2, self.pos, lax.rem(other, 2)))
+        self.far_peers = []
+        for step in range(1, self.far_count):
+            other = lax.rem(self.z + step, self.far_count)
+            self.far_peers.append((self.batch, other * 2 + self.core, self.ch))
+
+    @staticmethod
+    def scratch(width):
+        far = lax.axis_size("pos") // 2
+        count = 2 + 3 + far - 1
+        return [
+            pltpu.VMEM((8, width), F32),
+            pltpu.VMEM((8, width // 2), F32),
+            pltpu.VMEM((4, 8, width // 2), F32),
+            pltpu.VMEM((far, 8, width // 2), F32),
+            pltpu.VMEM((8, width), F32),
+            pltpu.SemaphoreType.DMA((count,)),
+            pltpu.SemaphoreType.DMA((count,)),
+        ]
+
+    def peers(self):
+        return [self.core_peer] + self.near_peers + self.far_peers
+
+    def copy(self, i, src, dst, peer):
+        return pltpu.make_async_remote_copy(
+            src, dst, self.send.at[i], self.recv.at[i], device_id=peer, device_id_type=MESH
+        )
+
+    def copies(self, stage):
+        if stage == 0:
+            return [self.copy(0, self.value.at[:, self.away], self.core_in, self.core_peer)]
+        if stage == 1:
+            slot = self.near.at[self.me]
+            return [self.copy(1 + i, slot, slot, p) for i, p in enumerate(self.near_peers)]
+        if stage == 2:
+            slot = self.far.at[self.z]
+            return [self.copy(4 + i, slot, slot, p) for i, p in enumerate(self.far_peers)]
+        part = self.result.at[:, self.mine]
+        return [self.copy(3 + self.far_count, part, part, self.core_peer)]
+
+    def wait(self, stage):
+        for copy in self.copies(stage):
+            copy.wait()
+
+    def start(self, stage):
+        if stage == 1:
+            self.wait(0)
+            self.near[pl.ds(self.me, 1)] = (self.value[:, self.mine] + self.core_in[...])[None]
+        if stage == 2:
+            self.wait(1)
+            total = (self.near[0] + self.near[1]) + (self.near[2] + self.near[3])
+            self.far[pl.ds(self.z, 1)] = total[None]
+        if stage == 3:
+            self.wait(2)
+            total = self.far[0]
+            for i in range(1, self.far_count):
+                total = total + self.far[i]
+            self.result[:, self.mine] = total
+        for copy in self.copies(stage):
+            copy.start()
+
+
+def meet(peers):
     barrier = pltpu.get_barrier_semaphore()
-    peers = []
-    for step in range(1, 4):
-        other = lax.rem(me + step, 4)
-        peers.append((other // 2, pos, lax.rem(other, 2)))
-    for step in range(1, pos_count):
-        peers.append((batch, lax.rem(pos + step, pos_count), ch))
     for peer in peers:
         pl.semaphore_signal(barrier, inc=1, device_id=peer, device_id_type=MESH)
-    near[pl.ds(me, 1)] = v_ref[...][None]
     pl.semaphore_wait(barrier, len(peers))
-    copies = [
-        pltpu.make_async_remote_copy(
-            v_ref, near.at[me], near_send.at[i], near_recv.at[i], device_id=peer, device_id_type=MESH
-        )
-        for i, peer in enumerate(peers[:3])
-    ]
-    for copy in copies:
-        copy.start()
-    for copy in copies:
-        copy.wait()
-    mid[...] = (near[0] + near[1]) + (near[2] + near[3])
-    far[pl.ds(pos, 1)] = mid[...][None]
-    copies = [
-        pltpu.make_async_remote_copy(
-            mid, far.at[pos], far_send.at[i], far_recv.at[i], device_id=peer, device_id_type=MESH
-        )
-        for i, peer in enumerate(peers[3:])
-    ]
-    for copy in copies:
-        copy.start()
-    for copy in copies:
-        copy.wait()
-    total = far[0]
-    for i in range(1, pos_count):
-        total = total + far[i]
-    o_ref[...] = total
+
+
+def reduce_kernel(v_ref, o_ref, *scratch):
+    value, core_in, near, far, result, send, recv = scratch
+    reduce = Reduce(value, core_in, near, far, result, (send, recv))
+    value[...] = v_ref[...]
+    meet(reduce.peers())
+    for stage in range(4):
+        reduce.start(stage)
+    reduce.wait(3)
+    o_ref[...] = result[...]
 
 
 def reduce_all(values, collective_id):
     rows, width = values.shape
-    padded = -(-rows // 8) * 8
-    values = jnp.pad(values, ((0, padded - rows), (0, 0)))
-    pos_count = lax.axis_size("pos")
-    shape = (padded, width)
     total = pl.pallas_call(
         reduce_kernel,
-        out_shape=jax.ShapeDtypeStruct(shape, F32),
+        out_shape=jax.ShapeDtypeStruct((8, width), F32),
         in_specs=[pl.BlockSpec(memory_space=pltpu.VMEM)],
         out_specs=pl.BlockSpec(memory_space=pltpu.VMEM),
-        scratch_shapes=[
-            pltpu.VMEM((4,) + shape, F32),
-            pltpu.VMEM(shape, F32),
-            pltpu.VMEM((pos_count,) + shape, F32),
-            pltpu.SemaphoreType.DMA((3,)),
-            pltpu.SemaphoreType.DMA((3,)),
-            pltpu.SemaphoreType.DMA((pos_count - 1,)),
-            pltpu.SemaphoreType.DMA((pos_count - 1,)),
-        ],
+        scratch_shapes=Reduce.scratch(width),
         compiler_params=params(collective_id=collective_id, has_side_effects=True),
-    )(values)
+        name="reduce",
+    )(jnp.pad(values, ((0, 8 - rows), (0, 0))))
     return total[:rows]
 
 
@@ -358,91 +400,403 @@
     )(first_own, first_other, vecs, w2, wp, out_grad, limits)
 
 
-def back_kernel(g_ref, wo_ref, wx_ref, x_ref, vec_ref, o_ref, s_ref):
-    micro_count, pairs = o_ref.shape[1:3]
-    half = wo_ref.shape[2]
-    sums = [[0.0, 0.0] for _ in range(micro_count)]
-    for e in range(2):
-        acc = 0.0
-        for k in range(KW):
-            d = e - k + KW - 1
-            acc += lax.dot_general(g_ref[d, :, :half], wo_ref[k], NT, preferred_element_type=F32)
-            acc += lax.dot_general(g_ref[d, :, half:], wx_ref[k], NT, preferred_element_type=F32)
+def tail_kernel(
+    scatter,
+    total_rows,
+    low,
+    hp,
+    gp,
+    wo,
+    wx,
+    xs_in,
+    vec_ref,
+    extra_ref,
+    ig,
+    dw_out,
+    sum_out,
+    g_buf,
+    w_buf,
+    a1g,
+    xs,
+    h_buf,
+    f_buf,
+    dw,
+    core_in,
+    x_in,
+    z_in,
+    dxs,
+    weave,
+    load_sem,
+    w_sem,
+    h_sem,
+    low_send,
+    low_recv,
+    core_send,
+    core_recv,
+    x_send,
+    x_recv,
+    z_send,
+    z_recv,
+    ig_send,
+    ig_recv,
+    ig_sem,
+    value,
+    r_core,
+    r_near,
+    r_far,
+    r_result,
+    r_send,
+    r_recv,
+):
+    reduce = Reduce(value, r_core, r_near, r_far, r_result, (r_send, r_recv))
+    batch, pos, ch, core, z = reduce.batch, reduce.pos, reduce.ch, reduce.core, reduce.z
+    far_count = reduce.far_count
+    chunks, rows_all, chunk = dw.shape
+    micro_count, half_rows, wide = dxs.shape
+    pairs = half_rows // 2
+    rows = micro_count * pairs
+    out = gp.shape[2]
+    local_out = out // 2
+    local_in = wide // 2
+    tile = w_buf.shape[2]
+    cut = h_buf.shape[3]
+    per_half = rows_all // 2 // cut
+    y_peer = (batch, pos, 1 - ch)
+    x_peer = (1 - batch, pos, ch)
+    core_peer = reduce.core_peer
+
+    def loads():
+        copies = [
+            pltpu.make_async_copy(gp, g_buf, load_sem.at[0]),
+            pltpu.make_async_copy(xs_in, xs, load_sem.at[1]),
+            pltpu.make_async_copy(low.at[:, :, 0:local_out], f_buf.at[0:2], load_sem.at[2]),
+        ]
+        return copies
+
+    def w_copies(j):
+        s = j % 2
+        at = slice(j * tile, (j + 1) * tile)
+        return [
+            pltpu.make_async_copy(wo.at[:, at, :], w_buf.at[s, :, :, 0:local_out], w_sem.at[s, 0]),
+            pltpu.make_async_copy(wx.at[:, at, :], w_buf.at[s, :, :, local_out:out], w_sem.at[s, 1]),
+        ]
+
+    def h_copies(side_half, t):
+        number = side_half * per_half + t
+        k = number // 2
+        at = pl.ds(pl.multiple_of(lax.rem(number, 2) * cut, cut), cut)
+        slot = lax.rem(t, 2)
+        return [
+            pltpu.make_async_copy(hp.at[s, k + e, :, at], h_buf.at[slot, 2 * s + e], h_sem.at[slot, 2 * s + e])
+            for s in range(2)
+            for e in range(2)
+        ]
+
+    def low_copy(c):
+        return pltpu.make_async_remote_copy(
+            low.at[:, :, local_out + c * chunk : local_out + (c + 1) * chunk],
+            f_buf.at[2:4, :, c * chunk : (c + 1) * chunk],
+            low_send.at[c],
+            low_recv.at[c],
+            device_id=y_peer,
+            device_id_type=MESH,
+        )
+
+    for copy in loads():
+        copy.start()
+    for copy in w_copies(0):
+        copy.start()
+    meet(reduce.peers())
+    low_copy(0).start()
+    for copy in h_copies(1 - batch, 0):
+        copy.start()
+    for copy in loads()[:2]:
+        copy.wait()
+    value[...] = extra_ref[...]
+
+    tiles = wide // tile
+
+    def back(j):
+        s = j % 2
+        if j + 1 < tiles:
+            for copy in w_copies(j + 1):
+                copy.start()
+        for copy in w_copies(j):
+            copy.wait()
+        at = slice(j * tile, (j + 1) * tile)
+        sums = [[0.0, 0.0] for _ in range(micro_count)]
+        for e in range(2):
+            acc = 0.0
+            for k in range(KW):
+                acc += lax.dot_general(
+                    g_buf[e - k + KW - 1], w_buf[s, k], NT, preferred_element_type=F32
+                )
+            for m in range(micro_count):
+                x = xs[e, m * pairs : (m + 1) * pairs, at].astype(F32)
+                moved = x - vec_ref[m, 0:1, at]
+                normed = moved * vec_ref[m, 3:4, at]
+                act = moved * vec_ref[m, 1:2, at] + vec_ref[m, 2:3, at]
+                grad = acc[m * pairs : (m + 1) * pairs] * gelu_slope(act)
+                a1g[e, m * pairs : (m + 1) * pairs, at] = grad
+                sums[m][0] += jnp.sum(grad, axis=0, keepdims=True)
+                sums[m][1] += jnp.sum(grad * normed, axis=0, keepdims=True)
         for m in range(micro_count):
-            x = x_ref[e, m].astype(F32)
-            normed = (x - vec_ref[m, 0:1, :]) * vec_ref[m, 3:4, :]
-            act = (x - vec_ref[m, 0:1, :]) * vec_ref[m, 1:2, :] + vec_ref[m, 2:3, :]
-            grad = acc[m * pairs : (m + 1) * pairs] * gelu_slope(act)
-            o_ref[e, m] = grad
-            sums[m][0] += jnp.sum(grad, axis=0, keepdims=True)
-            sums[m][1] += jnp.sum(grad * normed, axis=0, keepdims=True)
+            for i in range(2):
+                value[2 * m + i : 2 * m + i + 1, at] = sums[m][i]
+
+    block = rows_all // (2 * 2 * far_count)
+
+    def block_rows(side_half, zz, cc):
+        return pl.ds(pl.multiple_of(((side_half * far_count + zz) * 2 + cc) * block, 16), block)
+
+    def core_copy(c, kind, side_half, zz):
+        return pltpu.make_async_remote_copy(
+            dw.at[c, block_rows(side_half, zz, 1 - core)],
+            core_in.at[c, kind, zz],
+            core_send.at[c, kind, zz],
+            core_recv.at[c, kind, zz],
+            device_id=core_peer,
+            device_id_type=MESH,
+        )
+
+    def x_copy(c, zz):
+        return pltpu.make_async_remote_copy(
+            dw.at[c, block_rows(1 - batch, zz, core)],
+            x_in.at[c, zz],
+            x_send.at[c, zz],
+            x_recv.at[c, zz],
+            device_id=x_peer,
+            device_id_type=MESH,
+        )
+
+    def z_copy(c, r, zz):
+        return pltpu.make_async_remote_copy(
+            dw.at[c, block_rows(batch, zz, core)],
+            z_in.at[c, r],
+            z_send.at[c, r],
+            z_recv.at[c, r],
+            device_id=(batch, zz * 2 + core, ch),
+            device_id_type=MESH,
+        )
+
+    steps = list(range(far_count // 2, far_count)) + list(range(1, far_count // 2)) + [0]
+    if far_count == 4:
+        steps = [2, 1, 3, 0]
+
+    def away(r):
+        return lax.rem(z + steps[r], far_count)
+
+    def weigh(c, kind, side_half, following):
+        lanes = slice(c * chunk, (c + 1) * chunk)
+
+        @pl.loop(0, per_half)
+        def _(t):
+            @pl.when(t + 1 < per_half)
+            def _():
+                for copy in h_copies(side_half, t + 1):
+                    copy.start()
+
+            for copy in h_copies(side_half, t):
+                copy.wait()
+            slot = lax.rem(t, 2)
+            grad = lax.dot_general(
+                h_buf[slot].reshape(4 * rows, cut),
+                f_buf[:, :, lanes].reshape(4 * rows, chunk),
+                TN,
+                preferred_element_type=F32,
+            )
+            at = pl.multiple_of((side_half * per_half + t) * cut, 16)
+            dw[c, pl.ds(at, cut), :] = grad.astype(BF16)
+
+        if following is not None:
+            for copy in h_copies(following, 0):
+                copy.start()
+        if scatter:
+            for r in range(far_count):
+                core_copy(c, kind, side_half, away(r)).start()
+
+    def add_to(c, at, ref, *index):
+        dw[c, at, :] = (dw[c, at, :].astype(F32) + ref[index].astype(F32)).astype(BF16)
+
+    def send_x(c):
+        if scatter:
+            for r in range(far_count):
+                zz = away(r)
+                core_copy(c, 0, 1 - batch, zz).wait_recv()
+                add_to(c, block_rows(1 - batch, zz, core), core_in, c, 0, zz)
+                x_copy(c, zz).start()
+
+    def send_z(c):
+        if scatter:
+            for r in range(far_count):
+                zz = away(r)
+                core_copy(c, 1, batch, zz).wait_recv()
+                x_copy(c, zz).wait_recv()
+                at = block_rows(batch, zz, core)
+                total = dw[c, at, :].astype(F32) + core_in[c, 1, zz].astype(F32) + x_in[c, zz].astype(F32)
+                lanes = slice(c * chunk, (c + 1) * chunk)
+                if r < far_count - 1:
+                    dw[c, at, :] = total.astype(BF16)
+                    z_copy(c, r, zz).start()
+                else:
+                    dw_out[:, lanes] = total
+
+    def finish(c):
+        lanes = slice(c * chunk, (c + 1) * chunk)
+        if scatter:
+            for r in range(far_count - 1):
+                z_copy(c, r, away(r)).wait_recv()
+                dw_out[:, lanes] = dw_out[:, lanes] + z_in[c, r].astype(F32)
+        else:
+            copy = pltpu.make_async_copy(dw.at[c], dw_out.at[:, lanes], load_sem.at[3])
+            copy.start()
+            copy.wait()
+
+    def ig_remote(m):
+        at = pl.ds(pl.multiple_of(ch * half_rows, half_rows), half_rows)
+        lanes = pl.ds(pl.multiple_of((1 - ch) * local_in, 128), local_in)
+        return pltpu.make_async_remote_copy(
+            dxs.at[m, :, lanes], ig.at[m, at], ig_send.at[m], ig_recv.at[m], device_id=y_peer, device_id_type=MESH
+        )
+
+    def ig_local(m):
+        at = pl.ds(pl.multiple_of(ch * half_rows, half_rows), half_rows)
+        lanes = pl.ds(pl.multiple_of(ch * local_in, 128), local_in)
+        return pltpu.make_async_copy(dxs.at[m, :, lanes], ig.at[m, at], ig_sem.at[m])
+
+    def input_grad(m):
+        scale = 1.0 / total_rows
+
+        @pl.loop(0, wide // 128)
+        def _(b):
+            at = pl.ds(pl.multiple_of(b * 128, 128), 128)
+            plain = r_result[2 * m : 2 * m + 1, at] * scale
+            cross = r_result[2 * m + 1 : 2 * m + 2, at] * scale
+            inverse = vec_ref[m, 3:4, at]
+            for e in range(2):
+                x = xs[e, m * pairs : (m + 1) * pairs, at].astype(F32)
+                normed = (x - vec_ref[m, 0:1, at]) * inverse
+                grad = a1g[e, m * pairs : (m + 1) * pairs, at]
+                weave[pl.ds(e, pairs, stride=2), :] = vec_ref[m, 1:2, at] * (grad - plain - normed * cross)
+            dxs[m, :, at] = weave[...].astype(BF16)
+
+        ig_local(m).start()
+        ig_remote(m).start()
+
+    for j in range(2):
+        back(j)
+    loads()[2].wait()
+    low_copy(0).wait_recv()
+    for c in range(1, chunks):
+        low_copy(c).start()
+    weigh(0, 0, 1 - batch, batch)
+    send_x(0)
+    for j in range(2, tiles):
+        back(j)
+    reduce.start(0)
+    weigh(0, 1, batch, 1 - batch)
+    reduce.start(1)
+    low_copy(1).wait_recv()
+    weigh(1, 0, 1 - batch, batch)
+    send_x(1)
+    reduce.start(2)
+    send_z(0)
+    weigh(1, 1, batch, 1 - batch)
+    reduce.start(3)
+    low_copy(2).wait_recv()
+    weigh(2, 0, 1 - batch, batch)
+    send_x(2)
+    reduce.wait(3)
+    sum_out[...] = r_result[...]
     for m in range(micro_count):
-        for i in range(2):
-            s_ref[2 * m + i : 2 * m + i + 1, :] = sums[m][i]
-
-
-def conv_back(pieces, own, other, x, vecs, tile=256):
-    _, micro_count, pairs, out = pieces.shape
-    wide = own.shape[0] // KW
-    half = own.shape[1]
+        input_grad(m)
+    weigh(2, 1, batch, None)
+    send_z(1)
+    finish(0)
+    send_z(2)
+    finish(1)
+    finish(2)
+    for m in range(micro_count):
+        ig_local(m).wait()
+        ig_remote(m).wait()
+    for c in range(chunks):
+        low_copy(c).wait_send()
+        if scatter:
+            for r in range(far_count):
+                zz = away(r)
+                core_copy(c, 0, 1 - batch, zz).wait_send()
+                core_copy(c, 1, batch, zz).wait_send()
+                x_copy(c, zz).wait_send()
+                if r < far_count - 1:
+                    z_copy(c, r, zz).wait_send()
+
+
+def tail(low, pieces, grad_pieces, own, other, x_split, vecs, extra, total_rows):
+    sides, _, micro_count, pairs, wide = pieces.shape
     rows = micro_count * pairs
+    out = grad_pieces.shape[-1]
+    local_out = out // 2
+    chunks = 3
+    chunk = local_out // chunks
+    far = lax.axis_size("pos") // 2
+    rows_all = KW * wide
+    block = rows_all // (4 * far)
+    scatter = block % 16 == 0
+    tile = 256
+    land = block if scatter else 16
+    any_space = pl.BlockSpec(memory_space=pl.ANY)
+    in_vmem = pl.BlockSpec(memory_space=pltpu.VMEM)
+    dma = pltpu.SemaphoreType.DMA
     return pl.pallas_call(
-        back_kernel,
+        functools.partial(tail_kernel, scatter, total_rows),
         out_shape=(
-            jax.ShapeDtypeStruct((2, micro_count, pairs, wide), F32),
-            jax.ShapeDtypeStruct((8, wide), F32),
+            jax.ShapeDtypeStruct((micro_count, 4 * pairs, wide // 2), BF16),
+            jax.ShapeDtypeStruct((block, local_out) if scatter else (rows_all, local_out), F32 if scatter else BF16),
+            jax.ShapeDtypeStruct((8, out), F32),
         ),
-        grid=(wide // tile,),
-        in_specs=[
-            pl.BlockSpec((PIECES, rows, out), lambda j: (0, 0, 0)),
-            pl.BlockSpec((KW, tile, half), lambda j: (0, j, 0)),
-            pl.BlockSpec((KW, tile, half), lambda j: (0, j, 0)),
-            pl.BlockSpec((2, micro_count, pairs, tile), lambda j: (0, 0, 0, j)),
-            pl.BlockSpec((micro_count, 8, tile), lambda j: (0, 0, j)),
-        ],
-        out_specs=(
-            pl.BlockSpec((2, micro_count, pairs, tile), lambda j: (0, 0, 0, j)),
-            pl.BlockSpec((8, tile), lambda j: (0, j)),
-        ),
-        compiler_params=params(),
-        name="conv_back",
+        in_specs=[any_space] * 6 + [in_vmem] * 2,
+        out_specs=(any_space, in_vmem if scatter else any_space, in_vmem),
+        scratch_shapes=[
+            pltpu.VMEM((PIECES, rows, out), BF16),
+            pltpu.VMEM((2, KW, tile, out), BF16),
+            pltpu.VMEM((2, rows, wide), F32),
+            pltpu.VMEM((2, rows, wide), BF16),
+            pltpu.VMEM((2, 4, rows, wide // 2), BF16),
+            pltpu.VMEM((4, rows, local_out), BF16),
+            pltpu.VMEM((chunks, rows_all, chunk), BF16),
+            pltpu.VMEM((chunks, 2, far, land, chunk), BF16),
+            pltpu.VMEM((chunks, far, land, chunk), BF16),
+            pltpu.VMEM((chunks, far - 1, land, chunk), BF16),
+            pltpu.VMEM((micro_count, 2 * pairs, wide), BF16),
+            pltpu.VMEM((2 * pairs, 128), F32),
+            dma((4,)),
+            dma((2, 2)),
+            dma((2, 4)),
+            dma((chunks,)),
+            dma((chunks,)),
+            dma((chunks, 2, far)),
+            dma((chunks, 2, far)),
+            dma((chunks, far)),
+            dma((chunks, far)),
+            dma((chunks, far - 1)),
+            dma((chunks, far - 1)),
+            dma((micro_count,)),
+            dma((micro_count,)),
+            dma((micro_count,)),
+        ]
+        + Reduce.scratch(out),
+        compiler_params=params(collective_id=5, has_side_effects=True),
+        name="tail",
     )(
-        pieces.reshape(PIECES, rows, out),
-        own.reshape(KW, wide, half),
-        other.reshape(KW, wide, half),
-        x,
+        low.reshape(2, rows, out),
+        pieces.reshape(sides, PIECES, rows, wide),
+        grad_pieces.reshape(PIECES, rows, out),
+        own.reshape(KW, wide, local_out),
+        other.reshape(KW, wide, local_out),
+        x_split.reshape(2, rows, wide),
         vecs,
+        extra,
     )
-
-
-def weight_kernel(he_ref, ho_ref, f_ref, o_ref):
-    acc = 0.0
-    for s in range(f_ref.shape[0]):
-        acc += lax.dot_general(he_ref[s, 0], f_ref[s, 0], TN, preferred_element_type=F32)
-        acc += lax.dot_general(ho_ref[s, 0], f_ref[s, 1], TN, preferred_element_type=F32)
-    o_ref[...] = acc.astype(BF16)
-
-
-def conv_weight_grad(pieces, low, tile=256):
-    sides, _, micro_count, pairs, wide = pieces.shape
-    out = low.shape[-1]
-    rows = micro_count * pairs
-    pieces = pieces.reshape(sides, PIECES, rows, wide)
-    low = low.reshape(sides, 2, rows, out)
-    per = wide // tile
-    return pl.pallas_call(
-        weight_kernel,
-        out_shape=jax.ShapeDtypeStruct((KW * wide, out), BF16),
-        grid=(KW, per),
-        in_specs=[
-            pl.BlockSpec((sides, 1, rows, tile), lambda k, j: (0, k, 0, j)),
-            pl.BlockSpec((sides, 1, rows, tile), lambda k, j: (0, k + 1, 0, j)),
-            pl.BlockSpec((sides, 2, rows, out), lambda k, j: (0, 0, 0, 0)),
-        ],
-        out_specs=pl.BlockSpec((tile, out), lambda k, j: (k * per + j, 0)),
-        compiler_params=params(),
-        name="conv_weight_grad",
-    )(pieces, pieces, low)
 
 
 def local(
@@ -504,23 +858,15 @@
     x_full = natural(x_ext, other_ch(x_ext), 2)
 
     x32 = x.astype(F32)
-    lead = spot == 0
-    stats = jnp.concatenate(
-        [
-            jnp.sum(x32, axis=1),
-            jnp.sum(x32 * x32, axis=1),
-            jnp.where(lead, jnp.stack([norm1_gain, norm1_bias]), 0.0),
-        ]
-    )
+    stats = jnp.concatenate([jnp.sum(x32, axis=1), jnp.sum(x32 * x32, axis=1)])
+    stats = natural(stats, jnp.zeros_like(stats), 1)
+    moments = reduce_all(stats, 1) / total_rows
     small = jnp.stack([conv1_bias, norm2_gain, norm2_bias, conv2_bias])
-    small = jnp.where(lead, small, 0.0)
-    stats = natural(stats, jnp.zeros_like(stats), 1)
-    small = natural(small, jnp.zeros_like(small), 1)
-    stats = jnp.concatenate([stats, jnp.zeros((stats.shape[0], wide_out - wide_in), F32)], axis=1)
-    summed = reduce_all(jnp.concatenate([stats, small]), 1)
-    moments = summed[: 2 * micro_count, :wide_in] / total_rows
-    gain1, bias1 = summed[2 * micro_count, :wide_in], summed[2 * micro_count + 1, :wide_in]
-    small = summed[2 * micro_count + 2 :]
+    small = jnp.concatenate([small, jnp.pad(jnp.stack([norm1_gain, norm1_bias]), ((0, 0), (0, local_out - local_in)))])
+    small_other = other_ch(small)
+    gains1 = natural(small[4:, :local_in], small_other[4:, :local_in], 1)
+    gain1, bias1 = gains1[0], gains1[1]
+    small = jnp.concatenate([small[:4], small_other[:4]], axis=1)
     center1 = moments[:micro_count]
     inverse1 = lax.rsqrt(moments[micro_count:] - center1 * center1 + EPS)
 
@@ -529,7 +875,6 @@
             is_low, v, jnp.concatenate([v[..., local_out:], v[..., :local_out]], axis=-1)
         )
 
-    small = own_first(small)
     vec1 = jnp.stack(
         [center1, inverse1 * gain1, jnp.broadcast_to(bias1, center1.shape), inverse1]
         + [jnp.zeros_like(center1)] * 4,
@@ -603,11 +948,11 @@
     grad_pieces = jnp.stack(
         [longer[d % 2, :, d // 2 : d // 2 + pairs] for d in range(PIECES)]
     )
-    a1g, sums4 = conv_back(grad_pieces, conv1_weight, w1_other, x_split[0], vec1)
-
-    low_away = other_ch(first_low[..., local_out:])
-    low_both = jnp.stack([first_low[..., :local_out], low_away])
-    dw1 = conv_weight_grad(pieces, low_both)
+    extra = jnp.pad(to_natural(low_sum), ((2 * micro_count, 8 - 3 * micro_count), (0, 0)))
+    input_grad, dw1, part = tail(
+        first_low, pieces, grad_pieces, conv1_weight, w1_other, x_split[0], vec1, extra, total_rows
+    )
+    input_grad = input_grad.reshape(section_input.shape)
 
     def split_grad(left, right):
         left = own_first(left)
@@ -621,21 +966,11 @@
     def scatter(v):
         return lax.psum_scatter(v, ("batch", "pos"), scatter_dimension=0, tiled=True).astype(F32)
 
-    part = jnp.concatenate(
-        [sums4[: 2 * micro_count], jnp.zeros((2 * micro_count, wide_out - wide_in), F32)], axis=1
-    )
-    part = jnp.concatenate([part, to_natural(low_sum)])
-    part = reduce_all(part, 4)
     one = part[: 2 * micro_count, :wide_in]
     grad_sum, cross_sum = one[0::2], one[1::2]
-    normed1 = (x_split[0].astype(F32) - center1[None, :, None]) * inverse1[None, :, None]
-    dx = (inverse1 * gain1)[None, :, None] * (
-        a1g - (grad_sum / total_rows)[None, :, None] - normed1 * (cross_sum / total_rows)[None, :, None]
-    )
-    dx = jnp.stack([dx[0], dx[1]], axis=2).reshape(micro_count, half, wide_in).astype(BF16)
-    dx_own = lax.dynamic_slice_in_dim(dx, ch * local_in, local_in, axis=2)
-    dx_away = other_ch(lax.dynamic_slice_in_dim(dx, (1 - ch) * local_in, local_in, axis=2))
-    input_grad = natural(dx_own, dx_away, 1).reshape(section_input.shape)
+    low_sum = part[2 * micro_count : 3 * micro_count]
+    if dw1.shape[0] != KW * wide_in // plane:
+        dw1 = scatter(dw1)
 
     def mine_of(v, width):
         return lax.dynamic_slice_in_dim(v, ch * width, width, axis=0)
@@ -645,8 +980,8 @@
         input_grad,
         mine_of(jnp.sum(cross_sum, axis=0), local_in),
         mine_of(jnp.sum(grad_sum, axis=0), local_in),
-        scatter(dw1),
-        mine_of(jnp.sum(part[2 * micro_count :], axis=0), local_out),
+        dw1,
+        mine_of(jnp.sum(low_sum, axis=0), local_out),
         jnp.sum(sums3[:, 1], axis=0)[:local_out],
         jnp.sum(sums3[:, 0], axis=0)[:local_out],
         scatter(dw2),

time: 701 us -> 607 us (0.87)
  waiting for transfers between devices: 191 us -> 65.8 us
  Pallas kernels: 303 us -> 348 us
  other arithmetic: 66.8 us -> 54.6 us
    ppermute x10 -> x9, waiting for transfers between devices: 186 us -> 64.1 us  [other_ch(): return lax.ppermute(v, 'ch', swap)]
    pallas_call x6 -> x4, Pallas kernels: 212 us -> 258 us  [the longest x3 134 us: reduce_all(): pl.pallas_call(reduce_kernel, out_shape=jax.ShapeDtypeStruct((8, width),...]
    ppermute x10 -> x9, starting transfers between devices: 17.3 us -> 15.9 us  [other_ch(): return lax.ppermute(v, 'ch', swap)]
  transfers between devices with their start and end apart: 20 -> 18, of which waited for: 9 -> 5; matrix products, arithmetic and copies ran while one was open for 19% -> 18% of each run, Pallas kernels for 32% -> 47%
where the time goes in v2:
time: 607 us; the launch traced here: 596 us
  Pallas kernels  348 us (57%)
  local copies, waits for them, and re-layouts  79.1 us (13%)
  waiting for transfers between devices  65.8 us (11%)
  other arithmetic  54.6 us (9%)
  starting transfers between devices  25 us (4%)
  between operations  14.7 us (2%)
  matrix products  9.36 us (2%)
    pallas_call x3, Pallas kernels, reduce_all(): pl.pallas_call(reduce_kernel, out_shape=jax.ShapeDtypeStruct((8, width),...  134 us
    pallas_call x1, Pallas kernels, tail(): pl.pallas_call(functools.partial(tail_kernel, scatter, total_rows), out_s...  123 us
    ppermute x9, waiting for transfers between devices, other_ch(): return lax.ppermute(v, 'ch', swap)  64.1 us
    pallas_call x1, Pallas kernels, middle(): pl.pallas_call(middle_kernel, out_shape=(jax.ShapeDtypeStruct((micro_coun...  41.1 us
    pallas_call x2, Pallas kernels, conv_forward(): pl.pallas_call(conv_kernel, out_shape=(jax.ShapeDtypeStruct((2, micro_cou...  32.4 us
    pallas_call x1, Pallas kernels, make_hidden(): pl.pallas_call(hidden_kernel, out_shape=(jax.ShapeDtypeStruct((2, PIECES,...  16.6 us
    ppermute x9, starting transfers between devices, other_ch(): return lax.ppermute(v, 'ch', swap)  15.9 us
    concatenate x1, local copies, waits for them, and re-layouts, local(): x_ext = jnp.concatenate([before, x, after, pad], axis=1)  13 us
  transfers between devices with their start and end apart: 18, of which 5 were waited for; matrix products, arithmetic and copies ran while one was open for 18% of the time, Pallas kernels for 47%

profile of v2, /device:TPU:0, one launch (start us, length us, event | category | flops | bytes accessed | tf_op | source)
XLA Modules:
  0.0 596.5 jit_solution(4049243801774834384)
XLA Ops:
  8.3 3.0 collective-permute-start.5
  11.4 3.8 collective-permute-done.5
  18.7 3.4 collective-permute-done.6
  25.7 12.2 %collective-permute-done.4 = bf16[400,768]{1,0:T(8,128)(2,1)S(1)} collective-permute-done((bf16[400,768]{1,0:T(8,128)(2,1)S(1)}, bf16[400,768]{1,0:T(8,128)(2,1)S(1)}, u32[]{:S(2)}, u32[]{:S(2)}) %collective-permute-start.4) | collective-permute-done | bytes 614432 | tf_op jit(solution)/shard_map/ppermute | solution.py:832
  40.9 3.0 collective-permute-start
  49.6 2.5 dynamic-slice_bitcast_fusion.1
  56.6 13.0 %concatenate.124 = bf16[2,1040,640]{2,1,0:T(8,128)(2,1)S(1)} concatenate(bf16[2,2,640]{2,1,0:T(2,128)(2,1)S(1)} %collective-permute-done, bf16[2,1024,640]{2,1,0:T(8,128)(2,1)} %bitcast.55, bf16[2,2,640]{2,1,0:T(2,128)(2,1)S(1)} %collective-permute-done.1, bf16[2,12,640]{2,1,0:T(8,128)(2,1)S(1)} %broadcast_in_dim.16), dimensions={1} | concatenate | bytes 5324800 | tf_op jit(solution)/shard_map/concatenate | solution.py:857
  71.8 66.6 %reduce.16 = f32[8,1280]{1,0:T(8,128)} custom-call(f32[8,1280]{1,0:T(8,128)} %pad.22.v_ref), custom_call_target="tpu_custom_call" | custom-call | tf_op jit(solution)/shard_map/reduce/pallas_call | solution.py:137
  140.6 7.2 %maximum_select_fusion.3 = (bf16[1536,768]{1,0:T(8,128)(2,1)}, bf16[1536,768]{1,0:T(8,128)(2,1)}) fusion(bf16[1536,768]{1,0:T(8,128)(2,1)} %param.20, bf16[768,768]{1,0:T(8,128)(2,1)} %get-tuple-element.109, bf16[768,768]{1,0:T(8,128)(2,1)} %get-tuple-element.108, pred[]{:T(512)S(6)} %eq.16, bf16[1536,768]{1,0:T(8,128)(2,1)} %param.22, ...), kind=kLoop, calls=%fused_computation.30 | loop fusion | flops 11796480 | bytes 14155777 | tf_op jit(solution)/shard_map/jit(_where)/select_n | solution.py:904
  156.0 6.4 %maximum_select_fusion.x_ref = bf16[2,1040,1280]{2,1,0:T(8,128)(2,1)} fusion(bf16[2,1040,640]{2,1,0:T(8,128)(2,1)} %collective-permute-done.2, bf16[2,1040,640]{2,1,0:T(8,128)(2,1)S(1)} %concatenate.124, pred[]{:T(512)S(6)} %eq.16), kind=kLoop, calls=%fused_computation.16 | loop fusion | flops 23961600 | bytes 10649601 | tf_op jit(solution)/shard_map/jit(_where)/select_n | solution.py:835
  162.4 16.6 %hidden.1 = (bf16[2,6,2,256,1280]{4,3,2,1,0:T(8,128)(2,1)}, bf16[2,2,2,256,1280]{4,3,2,1,0:T(8,128)(2,1)}) custom-call(s32[3]{0:T(128)} %pad_add_fusion.who, bf16[2,1040,1280]{2,1,0:T(8,128)(2,1)} %maximum_select_fusion.x_ref, f32[2,8,1280]{2,1,0:T(8,128)} %stack.79.vec_ref), custom_call_target="tpu_custom_call" | custom-call | tf_op jit(solution)/shard_map/hidden/pallas_call | solution.py:192
  179.1 6.9 %slice.251 = bf16[1,6,2,256,1280]{4,3,2,1,0:T(8,128)(2,1)} slice(bf16[2,6,2,256,1280]{4,3,2,1,0:T(8,128)(2,1)} %get-tuple-element.28), slice={[0:1], [0:6], [0:2], [0:256], [0:1280]} | slice | bytes 15728640 | tf_op jit(solution)/shard_map/slice | solution.py:886
  186.0 16.3 %conv_forward.2 = (f32[2,2,256,768]{3,2,1,0:T(8,128)}, f32[8,768]{1,0:T(8,128)}) custom-call(bf16[6,512,1280]{2,1,0:T(8,128)(2,1)} %bitcast.47, bf16[6400,768]{1,0:T(8,128)(2,1)} %w_ref.1, f32[1,768]{1,0:T(1,128)} %copy-done.20), custom_call_target="tpu_custom_call" | custom-call | tf_op jit(solution)/shard_map/conv_forward/pallas_call | solution.py:242
  203.7 2.8 fusion.34
  217.4 16.1 %conv_forward.3 = (f32[2,2,256,768]{3,2,1,0:T(8,128)}, f32[8,768]{1,0:T(8,128)}) custom-call(bf16[6,512,1280]{2,1,0:T(8,128)(2,1)} %bitcast.48, bf16[6400,768]{1,0:T(8,128)(2,1)} %all-gather.4.cloned.1.call-done.w_ref, f32[1,768]{1,0:T(1,128)} %slice.322.b_ref), custom_call_target="tpu_custom_call" | custom-call | tf_op jit(solution)/shard_map/conv_forward/pallas_call | solution.py:242
  234.9 13.0 %reduce.17 = f32[8,1536]{1,0:T(8,128)} custom-call(f32[8,1536]{1,0:T(8,128)} %pad.24.v_ref), custom_call_target="tpu_custom_call" | custom-call | tf_op jit(solution)/shard_map/reduce/pallas_call | solution.py:137
  251.1 41.1 %middle.1 = (bf16[2,256,1536]{2,1,0:T(8,128)(2,1)}, bf16[2,512,1536]{2,1,0:T(8,128)(2,1)}, bf16[2,512,1536]{2,1,0:T(8,128)(2,1)}, bf16[2,256,1536]{2,1,0:T(8,128...) custom-call(f32[2,2,256,768]{3,2,1,0:T(8,128)} %get-tuple-element.29, ...), custom_call_target="tpu_custom_call" | custom-call | tf_op jit(solution)/shard_map/middle/pallas_call | solution.py:365
  296.0 5.1 convolution_bitcast_fusion.1
  301.2 3.5 copy-done.11
  308.2 3.4 slice.294
  312.3 54.8 %reduce.18 = f32[8,1536]{1,0:T(8,128)} custom-call(f32[8,1536]{1,0:T(8,128)} %pad.25.v_ref), custom_call_target="tpu_custom_call" | custom-call | tf_op jit(solution)/shard_map/reduce/pallas_call | solution.py:137
  368.9 5.1 fusion.10
  374.0 4.2 convolution_bitcast_fusion
  381.3 4.3 convert_reduce_fusion.1
  385.7 3.3 collective-permute-start.9
  389.1 44.6 %collective-permute-done.12 = bf16[1536,768]{1,0:T(8,128)(2,1)} collective-permute-done((bf16[1536,768]{1,0:T(8,128)(2,1)}, bf16[1536,768]{1,0:T(8,128)(2,1)}, u32[]{:S(2)}, u32[]{:S(2)}) %collective-permute-start.12) | collective-permute-done | bytes 2359328 | tf_op jit(solution)/shard_map/ppermute | solution.py:832
  433.7 3.9 fusion.9
  437.6 2.6 slice_bitcast_fusion
  444.0 2.7 collective-permute-start.8
  448.5 5.0 fusion
  453.5 123.4 %tail.1 = (bf16[2,1024,640]{2,1,0:T(8,128)(2,1)}, f32[400,768]{1,0:T(8,128)}, f32[8,1536]{1,0:T(8,128)}) custom-call(bf16[2,512,1536]{2,1,0:T(8,128)(2,1)} %bitcast.53, bf16[2,6,512,1280]{3,2,1,0:T(8,128)(2,1)} %bitcast.52, bf16[6,512,1536]{2,1,0:T(8,128)(2,1)} %bitcast.51, bf16[5,1280,768]{2,1,0:T(8,128)(2,1)} %bitcast.49, bf16[5,1280,768]{2,1,0:T(8,128)(2,1)} %bitcast.50, ...), custom_call_target="tpu_custom_call" | custom-call | tf_op jit(solution)/shard_map/tail/pallas_call | solution.py:750
  580.8 3.0 fusion.14
  (195 shorter events, 78.8 us)
Async XLA Ops:
  7.2 45.6 %copy-start.3 = (bf16[2,1,1024,640]{3,2,1,0:T(8,128)(2,1)S(1)}, bf16[2,1,1024,640]{3,2,1,0:T(8,128)(2,1)}, u32[]{:S(2)}) copy-start(bf16[2,1,1024,640]{3,2,1,0:T(8,128)(2,1)} %param.13) | copy-start | bytes 7864324
  7.2 196.5 %all-gather.6.cloned.1.call-start = ((), (), s32[]{:S(2)}) async-start(), calls=%async_computation.3 | async-start | bytes 2506752 | tf_op jit(solution)/shard_map/all_gather | solution.py:846
  8.3 6.9 %collective-permute-start.5 = (bf16[96,768]{1,0:T(8,128)(2,1)S(1)}, bf16[96,768]{1,0:T(8,128)(2,1)S(1)}, u32[]{:S(2)}, u32[]{:S(2)}) collective-permute-start(bf16[96,768]{1,0:T(8,128)(2,1)S(1)} %constant_dynamic-slice_fusion.1), channel_id=1, source_target_pairs={{0,1},{1,0},{2,3},{3,2},{4,5},{5,4},{6,7},{7,6},{8,9},{9,8},{10,11... | collective-permute-start | bytes 442376 | tf_op jit(solution)/shard_map/ppermute | solution.py:832
  15.9 190.6 %all-gather.8.cloned.1.call-start = ((), (), s32[]{:S(2)}) async-start(), calls=%async_computation.4 | async-start | bytes 2506752 | tf_op jit(solution)/shard_map/all_gather | solution.py:846
  16.9 5.2 collective-permute-start.6
  22.8 194.7 %all-gather.4.cloned.1.call-start = ((), (), s32[]{:S(2)}) async-start(), calls=%async_computation.2 | async-start | bytes 10444800 | tf_op jit(solution)/shard_map/all_gather | solution.py:846
  23.9 14.0 %collective-permute-start.4 = (bf16[400,768]{1,0:T(8,128)(2,1)S(1)}, bf16[400,768]{1,0:T(8,128)(2,1)S(1)}, u32[]{:S(2)}, u32[]{:S(2)}) collective-permute-start(bf16[400,768]{1,0:T(8,128)(2,1)S(1)} %constant_dynamic-slice_fusion.2), channel_id=1, source_target_pairs={{0,1},{1,0},{2,3},{3,2},{4,5},{5,4},{6,7},{7,6},{8,9},{9,8},{10,11... | collective-permute-start | bytes 1843208 | tf_op jit(solution)/shard_map/ppermute | solution.py:832
  38.8 545.0 %reduce-scatter.3.cloned.1.call-start = ((), (), s32[]{:S(2)}) async-start(), calls=%async_computation.5 | async-start | bytes 2506752 | tf_op jit(solution)/shard_map/reduce_scatter | solution.py:967
  39.6 17.0 %collective-permute-start.1 = (bf16[2,2,640]{2,1,0:T(2,128)(2,1)S(1)}, bf16[2,2,640]{2,1,0:T(2,128)(2,1)S(1)}, u32[]{:S(2)}, u32[]{:S(2)}) collective-permute-start(bf16[2,2,640]{2,1,0:T(2,128)(2,1)S(1)} %get-tuple-element.102), channel_id=1, source_target_pairs={{2,0},{4,2},{6,4},{8,6},{10,8},{12,10},{14,12},{3,1},{5,3},{7,5},{... | collective-permute-start | bytes 15368 | tf_op jit(solution)/shard_map/ppermute | solution.py:855
  40.9 15.7 %collective-permute-start = (bf16[2,2,640]{2,1,0:T(2,128)(2,1)S(1)}, bf16[2,2,640]{2,1,0:T(2,128)(2,1)S(1)}, u32[]{:S(2)}, u32[]{:S(2)}) collective-permute-start(bf16[2,2,640]{2,1,0:T(2,128)(2,1)S(1)} %get-tuple-element.103), channel_id=1, source_target_pairs={{0,2},{2,4},{4,6},{6,8},{8,10},{10,12},{12,14},{1,3},{3,5},{5,7},{... | collective-permute-start | bytes 15368 | tf_op jit(solution)/shard_map/ppermute | solution.py:854
  46.0 106.0 %copy-start.20 = (f32[1,768]{1,0:T(1,128)}, f32[1,768]{1,0:T(1,128)S(1)}, u32[]{:S(2)}) copy-start(f32[1,768]{1,0:T(1,128)S(1)} %stack.72.b_ref) | copy-start | bytes 9220
  46.7 8.3 %copy-start.23 = (f32[1,768]{1,0:T(1,128)}, f32[1,768]{1,0:T(1,128)S(1)}, u32[]{:S(2)}) copy-start(f32[1,768]{1,0:T(1,128)S(1)} %stack.73) | copy-start | bytes 9220
  47.4 7.6 %copy-start.24 = (f32[1,768]{1,0:T(1,128)}, f32[1,768]{1,0:T(1,128)S(1)}, u32[]{:S(2)}) copy-start(f32[1,768]{1,0:T(1,128)S(1)} %stack.74) | copy-start | bytes 9220
  48.1 100.2 %collective-permute-start.3 = (f32[6,768]{1,0:T(8,128)S(1)}, f32[6,768]{1,0:T(8,128)}, u32[]{:S(2)}, u32[]{:S(2)}) collective-permute-start(f32[6,768]{1,0:T(8,128)S(1)} %concatenate.130), channel_id=1, source_target_pairs={{0,1},{1,0},{2,3},{3,2},{4,5},{5,4},{6,7},{7,6},{8,9},{9,8},{10,11... | collective-permute-start | bytes 55304 | tf_op jit(solution)/shard_map/ppermute | solution.py:832
  52.2 101.4 %collective-permute-start.7 = (bf16[2,256,768]{2,1,0:T(8,128)(2,1)}, bf16[2,256,768]{2,1,0:T(8,128)(2,1)}, u32[]{:S(2)}, u32[]{:S(2)}) collective-permute-start(bf16[2,256,768]{2,1,0:T(8,128)(2,1)} %get-tuple-element.117), channel_id=1, source_target_pairs={{0,1},{1,0},{2,3},{3,2},{4,5},{5,4},{6,7},{7,6},{8,9},{9,8},{10,11... | collective-permute-start | bytes 2359304 | tf_op jit(solution)/shard_map/ppermute | solution.py:832
  69.7 86.3 %collective-permute-start.2 = (bf16[2,1040,640]{2,1,0:T(8,128)(2,1)S(1)}, bf16[2,1040,640]{2,1,0:T(8,128)(2,1)}, u32[]{:S(2)}, u32[]{:S(2)}) collective-permute-start(bf16[2,1040,640]{2,1,0:T(8,128)(2,1)S(1)} %concatenate.124), channel_id=1, source_target_pairs={{0,1},{1,0},{2,3},{3,2},{4,5},{5,4},{6,7},{7,6},{8,9},{9,8},{10,11... | collective-permute-start | bytes 7987208 | tf_op jit(solution)/shard_map/ppermute | solution.py:832
  217.4 16.8 %copy-start.21 = (f32[4,768]{1,0:T(4,128)S(1)}, f32[4,768]{1,0:T(4,128)}, u32[]{:S(2)}) copy-start(f32[4,768]{1,0:T(4,128)} %slice.253) | copy-start | bytes 36868
  217.4 32.2 %copy-start.22 = (f32[1536]{0:T(1024)S(1)}, f32[1536]{0:T(1024)}, u32[]{:S(2)}) copy-start(f32[1536]{0:T(1024)} %get-tuple-element.83) | copy-start | bytes 18436
  217.4 33.0 %copy-start.27 = (f32[2]{0:T(128)S(1)}, f32[2]{0:T(128)}, u32[]{:S(2)}) copy-start(f32[2]{0:T(128)} %fusion.23) | copy-start | bytes 28
  306.4 62.3 %copy-start.10 = (bf16[2,256,1536]{2,1,0:T(8,128)(2,1)S(1)}, bf16[2,256,1536]{2,1,0:T(8,128)(2,1)}, u32[]{:S(2)}) copy-start(bf16[2,256,1536]{2,1,0:T(8,128)(2,1)} %get-tuple-element.43) | copy-start | bytes 4718596
  306.4 62.4 %collective-permute-start.11 = (bf16[1536,768]{1,0:T(8,128)(2,1)}, bf16[1536,768]{1,0:T(8,128)(2,1)}, u32[]{:S(2)}, u32[]{:S(2)}) collective-permute-start(bf16[1536,768]{1,0:T(8,128)(2,1)} %slice.388), channel_id=1, source_target_pairs={{0,1},{1,0},{2,3},{3,2},{4,5},{5,4},{6,7},{7,6},{8,9},{9,8},{10,11... | collective-permute-start | bytes 7077896 | tf_op jit(solution)/shard_map/ppermute | solution.py:832
  373.9 211.5 %reduce-scatter.5.cloned.1.call-start = ((), (), s32[]{:S(2)}) async-start(), calls=%async_computation.6 | async-start | bytes 2506752 | tf_op jit(solution)/shard_map/reduce_scatter | solution.py:967
  374.0 7.3 %slice-start = ((s8[6291456]{0:T(1024)(128)(4,1)}), s8[4194304]{0:T(1024)(128)(4,1)S(1)}, s32[]{:S(2)}) async-start(s8[6291456]{0:T(1024)(128)(4,1)} %bitcast.57), calls=%async_computation.7 | async-start | bytes 8388608
  374.0 7.2 %copy-start.2 = (f32[2,2,256,768]{3,2,1,0:T(8,128)S(1)}, f32[2,2,256,768]{3,2,1,0:T(8,128)}, u32[]{:S(2)}) copy-start(f32[2,2,256,768]{3,2,1,0:T(8,128)} %get-tuple-element.30.fx_ref) | copy-start | bytes 9437188
  374.0 7.2 %slice-start.1 = ((s8[6291456]{0:T(1024)(128)(4,1)}), s8[2097152]{0:T(1024)(128)(4,1)S(1)}, s32[]{:S(2)}) async-start(s8[6291456]{0:T(1024)(128)(4,1)} %bitcast.57), calls=%async_computation.8 | async-start | bytes 4194304
  379.9 53.8 %collective-permute-start.12 = (bf16[1536,768]{1,0:T(8,128)(2,1)}, bf16[1536,768]{1,0:T(8,128)(2,1)}, u32[]{:S(2)}, u32[]{:S(2)}) collective-permute-start(bf16[1536,768]{1,0:T(8,128)(2,1)} %slice.387), channel_id=1, source_target_pairs={{0,1},{1,0},{2,3},{3,2},{4,5},{5,4},{6,7},{7,6},{8,9},{9,8},{10,11... | collective-permute-start | bytes 7077896 | tf_op jit(solution)/shard_map/ppermute | solution.py:832
  385.6 62.9 %copy-start = (bf16[2,2,256,1536]{3,2,1,0:T(8,128)(2,1)}, bf16[2,2,256,1536]{3,2,1,0:T(8,128)(2,1)S(1)}, u32[]{:S(2)}) copy-start(bf16[2,2,256,1536]{3,2,1,0:T(8,128)(2,1)S(1)} %get-tuple-element.89) | copy-start | bytes 9437188
  385.7 60.9 %collective-permute-start.9 = (bf16[2,2,1,1536]{3,2,1,0:T(2,128)(2,1)S(1)}, bf16[2,2,1,1536]{3,2,1,0:T(2,128)(2,1)S(1)}, u32[]{:S(2)}, u32[]{:S(2)}) collective-permute-start(bf16[2,2,1,1536]{3,2,1,0:T(2,128)(2,1)S(1)} %get-tuple-element.96), channel_id=1, source_target_pairs={{0,1},{1,2},{2,3},{3,4},{4,5},{5,6},{6,7},{7,8},{8,9},{9,10},{10,1... | collective-permute-start | bytes 36872 | tf_op jit(solution)/shard_map/ppermute | solution.py:945
  442.7 5.7 collective-permute-start.10
  444.0 136.8 %collective-permute-start.8 = (bf16[2,256,768]{2,1,0:T(8,128)(2,1)}, bf16[2,256,768]{2,1,0:T(8,128)(2,1)}, u32[]{:S(2)}, u32[]{:S(2)}) collective-permute-start(bf16[2,256,768]{2,1,0:T(8,128)(2,1)} %get-tuple-element.115), channel_id=1, source_target_pairs={{0,1},{1,0},{2,3},{3,2},{4,5},{5,4},{6,7},{7,6},{8,9},{9,8},{10,11... | collective-permute-start | bytes 2359304 | tf_op jit(solution)/shard_map/ppermute | solution.py:832
  453.5 127.3 %copy-start.14 = (bf16[2,1,256,768]{3,2,0,1:T(8,128)(2,1)S(1)}, bf16[2,1,256,768]{3,2,0,1:T(8,128)(2,1)}, u32[]{:S(2)}) copy-start(bf16[2,1,256,768]{3,2,0,1:T(8,128)(2,1)} %get-tuple-element.114) | copy-start | bytes 2359300
  576.9 10.3 %copy-start.15 = (bf16[2,1024,640]{2,1,0:T(8,128)(2,1)S(1)}, bf16[2,1024,640]{2,1,0:T(8,128)(2,1)}, u32[]{:S(2)}) copy-start(bf16[2,1024,640]{2,1,0:T(8,128)(2,1)} %get-tuple-element.38) | copy-start | bytes 7864324
  (17 other events, 48.3 us)
Sparse Core Ops, SparseCore 0:
  16.0 43.6 all-gather.5
  62.6 41.0 all-gather.7
  106.1 84.3 all-gather.3
  374.1 61.7 reduce-scatter.2
  439.9 63.1 reduce-scatter.4
